TPU v7x, 128 devices: a whole 4x4x4 slice. The times are simulated.
128 devices in a mesh: fsdp: 16 (over x, z_hi, core), seq: 8 (over z_lo, y).
Axes of the slice: x: 4, y: 4, z: 4 (z_hi: 2, z_lo: 2; z = z_hi * 2 + z_lo), core: 2. Of those that a mesh axis runs over, the one named last changes fastest.
Arguments:
- incoming_hidden_state: bfloat16 [16, 1024, 3072], P('fsdp', 'seq'), may hold values from -6 to 6
- projected_queries: bfloat16 [16, 1024, 3072], P('fsdp', 'seq'), may hold values from -120 to 120
- projected_keys: bfloat16 [16, 1024, 3072], P('fsdp', 'seq'), may hold values from -6.1 to 6.1
- projected_values: bfloat16 [16, 1024, 3072], P('fsdp', 'seq'), may hold values from -6 to 6
- training_noise: bfloat16 [16, 1024, 3072], P('fsdp', 'seq'), may hold values from -6 to 6
- group_trajectory_counts: int32 [4], replicated, may hold values from 1 to 8, 16 in all
- timestep: int32 [16], replicated, may hold values from 0 to 15
- block_shard_owner: int32 [16, 128, 1], P('fsdp', 'seq'), may hold values from 0 to 15; in each aligned block of 16 rows (0 to 15, 16 to 31, ..., all dimensions but the last counted through in order) at most 3 rows name the same one
- frozen_weight: bfloat16 [3072, 3072], P('fsdp'), may hold values from -0.109375 to 0.109375
- adapter_down_weight: bfloat16 [3072, 128], P('fsdp'), may hold values from -0.109375 to 0.109375
- adapter_up_weight: bfloat16 [3072, 128], P('fsdp'), may hold values from -0.5 to 0.5
- linear_reward_head: float32 [3072], replicated, may hold values from -0.109375 to 0.109375
Outputs:
- final: bfloat16 [16, 1024, 3072], P('fsdp', 'seq')
- grad_down: float32 [3072, 128], P(('fsdp', 'seq'))
- grad_up: float32 [3072, 128], P(('fsdp', 'seq'))
- device_token_loss: float32 [16, 8], P('fsdp', 'seq')
Inputs may be any that keep to these rules, and one draw needn't show every extreme that they name: `block_shard_owner`: among the 16 blocks of one device at most 3 have the same owner, and exactly 3 in some device. `group_trajectory_counts`: they sum to 16; the largest is 8.
All inputs are finite; a program needn't handle non-finite values.
Results may differ from a plain program's by a relative error of at most 0.013.
Values may be sent and summed in bfloat16 or wider, within the bound.
A program may use at most 128 MiB of HBM per device.

v0:
```python
import math

import jax
import jax.numpy as jnp
from jax import lax
from jax.sharding import PartitionSpec as P

HEAD_FEATURES = 128
TOKENS_DEV = 128
ROWS_PER_BLOCK = 8
SAMPLE_STEPS = 16


adapter_scale = 2.0
adv_floor = 0.5
norm_eps = 1e-06


def noise_levels(timestep):
    level = 1.0 - timestep.astype(jnp.float32) / SAMPLE_STEPS
    return 5.0 * level / (1.0 + 4.0 * level)


def advantages(rewards, group_trajectory_counts):
    count_traj = rewards.shape[0]
    bounds = jnp.cumsum(group_trajectory_counts)
    members = jnp.sum(
        (bounds[None, :] <= jnp.arange(count_traj)[:, None]).astype(jnp.int32), axis=1
    )
    onehot = (members[:, None] == jnp.arange(group_trajectory_counts.shape[0])[None, :]).astype(
        jnp.float32
    )
    counts = jnp.sum(onehot, axis=0)
    group_means = jnp.sum(onehot * rewards[:, None], axis=0) / counts
    spread = rewards - jnp.sum(onehot * group_means[None, :], axis=1)
    variance = jnp.sum(onehot * (spread * spread)[:, None], axis=0) / counts
    deviation = jnp.sum(onehot * jnp.sqrt(variance)[None, :], axis=1)
    return spread / jnp.maximum(deviation, adv_floor)


def per_device(
    incoming_hidden_state,
    projected_queries,
    projected_keys,
    projected_values,
    training_noise,
    group_trajectory_counts,
    timestep,
    block_shard_owner,
    frozen_weight,
    adapter_down_weight,
    adapter_up_weight,
    linear_reward_head,
):
    rows_local = incoming_hidden_state.shape[1]
    features = incoming_hidden_state.shape[2]
    heads = features // HEAD_FEATURES
    seq_devices = lax.axis_size("seq")
    fsdp_devices = lax.axis_size("fsdp")
    seq_length = rows_local * seq_devices
    score_scale = 1.0 / math.sqrt(HEAD_FEATURES)
    query_head_split = projected_queries[0].reshape(rows_local, heads, HEAD_FEATURES)
    pieces = (
        lax.all_gather(projected_keys, "seq", axis=1, tiled=True),
        lax.all_gather(projected_values, "seq", axis=1, tiled=True),
    )
    running_max = jnp.full((heads, rows_local), -1e30, jnp.float32)
    piece_rows = pieces[0].shape[1]
    key_head_split = pieces[0][0].reshape(piece_rows, heads, HEAD_FEATURES)
    value_head_split = pieces[1][0].reshape(piece_rows, heads, HEAD_FEATURES)
    attention_scores = (
        jnp.einsum(
            "shd,nhd->hsn", query_head_split, key_head_split, preferred_element_type=jnp.float32
        )
        * score_scale
    )
    new_max = jnp.maximum(running_max, jnp.max(attention_scores, axis=2))
    expo = jnp.exp(attention_scores - new_max[:, :, None])
    new_sum = jnp.sum(expo, axis=2)
    update = jnp.einsum(
        "hsn,nhd->shd",
        expo.astype(jnp.bfloat16),
        value_head_split,
        preferred_element_type=jnp.float32,
    )
    attention = (update / jnp.transpose(new_sum)[:, :, None]).reshape(rows_local, features)
    final = (incoming_hidden_state[0].astype(jnp.float32) + attention).astype(jnp.bfloat16)
    partial_reward = jnp.sum(final.astype(jnp.float32) * linear_reward_head[None, :]) / math.sqrt(
        seq_length
    )
    trajectory_reward = lax.psum(partial_reward, "seq")
    rewards = lax.all_gather(trajectory_reward.reshape(1), "fsdp", axis=0, tiled=True)
    advantage = advantages(rewards, group_trajectory_counts)
    sigma = noise_levels(timestep)
    block_count = rows_local // ROWS_PER_BLOCK
    capacity = 3 * block_count // fsdp_devices
    owners = block_shard_owner[0, :, 0]
    owner_hot = (owners[:, None] == jnp.arange(fsdp_devices)[None, :]).astype(jnp.int32)
    earlier = jnp.cumsum(owner_hot, axis=0) - owner_hot
    slot_index = owners * capacity + jnp.sum(earlier * owner_hot, axis=1)
    placing = (slot_index[None, :] == jnp.arange(fsdp_devices * capacity)[:, None]).astype(
        jnp.bfloat16
    )

    def place(token_rows):
        packed = jnp.dot(
            placing,
            token_rows.reshape(block_count, ROWS_PER_BLOCK * features),
            preferred_element_type=jnp.float32,
        )
        return packed.astype(jnp.bfloat16).reshape(
            fsdp_devices, capacity * ROWS_PER_BLOCK, features
        )

    got_final, got_noise = (
        lax.all_to_all(place(final), "fsdp", split_axis=0, concat_axis=0, tiled=True),
        lax.all_to_all(place(training_noise[0]), "fsdp", split_axis=0, concat_axis=0, tiled=True),
    )
    slot_rows = capacity * ROWS_PER_BLOCK
    level_rows = jnp.repeat(sigma, slot_rows)[:, None]
    weight_rows = jnp.repeat(advantage, slot_rows)[:, None]
    latent = got_final.reshape(fsdp_devices * slot_rows, features).astype(jnp.float32)
    fresh = got_noise.reshape(fsdp_devices * slot_rows, features).astype(jnp.float32)
    noised_latent = ((1.0 - level_rows) * latent + level_rows * fresh).astype(jnp.bfloat16)
    target = fresh - latent
    adapter_width = adapter_down_weight.shape[1]
    pieces = (
        lax.all_gather(frozen_weight, "fsdp", axis=0, tiled=True),
        lax.all_gather(adapter_down_weight, "fsdp", axis=0, tiled=True),
    )
    frozen_output = jnp.dot(noised_latent, pieces[0], preferred_element_type=jnp.float32)
    lowrank_f = jnp.dot(noised_latent, pieces[1], preferred_element_type=jnp.float32)
    complete_up_weight = lax.all_gather(adapter_up_weight, "fsdp", axis=0, tiled=True)
    rank_projection = lowrank_f.astype(jnp.bfloat16)
    predicted_velocity = frozen_output + adapter_scale * jnp.einsum(
        "rk,fk->rf", rank_projection, complete_up_weight, preferred_element_type=jnp.float32
    )
    error = predicted_velocity - target
    token_loss = weight_rows[:, 0] * jnp.mean(error * error, axis=1)
    device_token_loss = (jnp.sum(token_loss) / TOKENS_DEV).reshape(1, 1)
    velocity_target = (weight_rows * error / seq_length).astype(jnp.bfloat16)
    backward_function = (
        adapter_scale
        * jnp.dot(velocity_target, complete_up_weight, preferred_element_type=jnp.float32)
    ).astype(jnp.bfloat16)
    down_local = jnp.einsum(
        "rf,rk->fk", noised_latent, backward_function, preferred_element_type=jnp.float32
    )
    shard_up_weight = adapter_scale * jnp.einsum(
        "rf,rk->fk", velocity_target, rank_projection, preferred_element_type=jnp.float32
    )
    local_grads = jnp.concatenate([down_local, shard_up_weight], axis=1)
    own_square = jnp.sum(local_grads * local_grads)
    square_total = lax.psum(own_square, ("fsdp", "seq"))
    limit = jnp.sqrt(square_total / (fsdp_devices * seq_devices) + norm_eps)
    clip_factor = limit / jnp.maximum(jnp.sqrt(own_square), limit)
    stacked_rows = lax.psum_scatter(
        clip_factor * local_grads, ("fsdp", "seq"), scatter_dimension=0, tiled=True
    )
    return (
        final[None],
        stacked_rows[:, :adapter_width],
        stacked_rows[:, adapter_width:],
        device_token_loss,
    )


def solution(mesh):
    return jax.shard_map(
        per_device,
        mesh=mesh,
        in_specs=(
            P("fsdp", "seq", None),
            P("fsdp", "seq", None),
            P("fsdp", "seq", None),
            P("fsdp", "seq", None),
            P("fsdp", "seq", None),
            P(),
            P(),
            P("fsdp", "seq", None),
            P("fsdp", None),
            P("fsdp", None),
            P("fsdp", None),
            P(),
        ),
        out_specs=(
            P("fsdp", "seq", None),
            P(("fsdp", "seq"), None),
            P(("fsdp", "seq"), None),
            P("fsdp", "seq"),
        ),
        check_vma=False,
    )
```

profile of v0, /device:TPU:0, one launch (start us, length us, event | category | flops | bytes accessed | tf_op | source)
XLA Modules:
  0.0 1122.5 jit_solution(6930621863481943980)
XLA Ops:
  7.2 0.7 all-gather.6.cloned.1.call-update
  8.0 2.3 copy.40
  10.3 0.7 all-gather.8.cloned.1.call-update
  11.0 0.4 reshape_squeeze.15
  11.5 0.2 select_reduce_fusion
  11.7 0.8 convolution_convert_fusion
  12.5 2.5 reshape.113
  15.0 7.9 all-to-all-start.1
  22.9 1.4 copy.46
  24.4 1.5 reshape.118
  25.9 1.3 copy.54
  27.1 76.4 %all-gather.6.cloned.1.call-done = bf16[1,1024,3072]{2,1,0:T(8,128)(2,1)} async-done(((bf16[1,128,3072]{2,1,0:T(8,128)(2,1)}), bf16[1,1024,3072]{2,1,0:T(8,128)(2,1)}) %all-gather.6.cloned.1.call-update) | async-done | bytes 6291472 | tf_op jit(solution)/shard_map/all_gather | solution.py:65
  103.6 8.7 copy.43
  112.2 70.7 %all-gather.4.cloned.1.call-done = bf16[1,1024,3072]{1,2,0:T(8,128)(2,1)} async-done(((bf16[1,128,3072]{1,2,0:T(8,128)(2,1)}), bf16[1,1024,3072]{1,2,0:T(8,128)(2,1)}) %all-gather.4.cloned.1.call-update) | async-done | bytes 6291472 | tf_op jit(solution)/shard_map/all_gather | solution.py:64
  183.0 4.7 multiply_reduce_fusion
  187.7 2.8 fusion
  190.5 1.8 copy-done
  192.2 12.4 %multiply_reduce_fusion.3 = (f32[]{:T(128)}, f32[128,24,128]{0,2,1:T(8,128)}) fusion(f32[128,24,128]{0,2,1:T(8,128)} %bitcast.42, f32[24,128]{1,0:T(8,128)S(1)} %bitcast.47, f32[128,24]{0,1:T(8,128)S(1)} %bitcast.44, bf16[1024,24,128]{0,2,1:T(8,128)(2,1)} %bitcast.40, f32[24,128,1024]{2,1,0:T(8,128)} %copy-done, f32[24,128]{1,0:T(8,128)S(1)} %broadcast_maximum_fusion), kind=kOutput, calls=%fused_computation.22 | convolution fusion | flops 817102848 | bytes 22056964 | tf_op jit(solution)/shard_map/hsn,nhd->shd/dot_general | solution.py:80
  204.6 3.0 copy.45
  207.7 2.9 reshape.111
  210.6 4.0 convolution_convert_fusion.1
  214.6 4.5 reshape.112
  219.1 6.7 all-to-all-start
  226.1 0.2 reduce-window.8
  226.2 0.6 dynamic-slice
  226.9 63.7 %all_gather.22 = bf16[3072,128]{1,0:T(8,128)(2,1)} all-gather(bf16[192,128]{1,0:T(8,128)(2,1)S(1)} %copy-done.9), channel_id=1, replica_groups=mesh['fsdp'=16,'seq'=8] {'fsdp'}, dimensions={0}, use_global_device_ids=true | all-gather | bytes 835584 | tf_op jit(solution)/shard_map/all_gather | solution.py:129
  290.6 27.3 %all_gather.23 = bf16[3072,128]{1,0:T(8,128)(2,1)S(1)} all-gather(bf16[192,128]{1,0:T(8,128)(2,1)S(1)} %copy-done.10), channel_id=1, replica_groups=mesh['fsdp'=16,'seq'=8] {'fsdp'}, dimensions={0}, use_global_device_ids=true | all-gather | bytes 835584 | tf_op jit(solution)/shard_map/all_gather | solution.py:133
  318.6 19.9 %psum.14 = f32[1]{0:T(128)} all-reduce(f32[1]{0:T(128)} %bitcast.10), channel_id=1, replica_groups=mesh['fsdp'=16,'seq'=8] {'seq'}, use_global_device_ids=true, to_apply=%region_5.6 | all-reduce | flops 1 | bytes 8 | tf_op jit(solution)/shard_map/psum | solution.py:91
  338.5 1.4 dynamic-update-slice
  339.9 33.3 %all-reduce = f32[16]{0:T(128)S(1)} all-reduce(f32[16]{0:T(128)S(1)} %dynamic-update-slice), channel_id=1, replica_groups=mesh['fsdp'=16,'seq'=8] {'fsdp'}, use_global_device_ids=true, to_apply=%add | all-reduce | flops 16 | bytes 128
  373.9 3.1 fusion.7
  377.0 1.4 copy-done.2
  378.4 0.8 convolution_convert_fusion.2
  379.2 11.5 %fusion.24 = f32[384,3072]{1,0:T(8,128)S(1)} fusion(bf16[384,3072]{1,0:T(8,128)(2,1)} %copy-done.2, bf16[3072,3072]{1,0:T(8,128)(2,1)} %all-gather.8.cloned.1.call-done), kind=kOutput, calls=%fused_computation.59 | convolution fusion | flops 7247757312 | bytes 25952256 | tf_op jit(solution)/shard_map/dot_general | solution.py:131
  390.8 3.2 multiply_reduce_fusion.1
  394.0 2.1 copy-done.1
  396.1 0.7 convolution_multiply_fusion
  396.8 5.4 fusion.13
  402.2 1.4 multiply_reduce_fusion.2
  403.6 63.2 %psum.15 = f32[]{:T(128)} all-reduce(f32[]{:T(128)} %multiply_reduce_fusion.2), channel_id=1, replica_groups=mesh['fsdp'=16,'seq'=8] {'fsdp','seq'}, use_global_device_ids=true, to_apply=%region_14.15 | all-reduce | flops 1 | bytes 8 | tf_op jit(solution)/shard_map/psum | solution.py:154
  468.2 1.9 fusion.9
  470.1 3.5 copy.50
  473.7 1.4 copy-done.6
  475.1 1.6 copy.44
  476.9 2.4 add_convert_fusion.2
  479.3 0.6 multiply_reduce_fusion.4
  480.6 632.9 %reduce-scatter.4.cloned.1.call-done = f32[24,256]{1,0:T(8,128)} async-done(((f32[3072,256]{1,0:T(8,128)}), f32[24,256]{1,0:T(8,128)}) %reduce-scatter.4.cloned.1.call-update) | async-done | bytes 24592
  1113.5 1.3 fusion.23
  (59 shorter events, 1.5 us)
Async XLA Ops:
  7.2 3.9 copy-start.7
  7.2 4.2 copy-start.11
  7.2 96.4 %all-gather.6.cloned.1.call-start = ((), (), s32[]{:S(2)}) async-start(), calls=%async_computation.4 | async-start | bytes 7077888 | tf_op jit(solution)/shard_map/all_gather | solution.py:65
  7.9 175.1 %all-gather.4.cloned.1.call-start = ((), (), s32[]{:S(2)}) async-start(), calls=%async_computation.3 | async-start | bytes 7077888 | tf_op jit(solution)/shard_map/all_gather | solution.py:64
  10.3 368.9 %all-gather.8.cloned.1.call-start = ((), (), s32[]{:S(2)}) async-start(), calls=%async_computation.5 | async-start | bytes 20054016 | tf_op jit(solution)/shard_map/all_gather | solution.py:128
  15.0 7.9 copy-start.4
  15.0 204.1 %all-to-all-start.1 = ((bf16[16,24,3072]{2,1,0:T(8,128)(2,1)}), bf16[16,24,3072]{2,1,0:T(8,128)(2,1)S(1)}, u32[]{:S(2)}, u32[]{:S(2)}) async-start(bf16[16,24,3072]{2,1,0:T(8,128)(2,1)} %reshape.113), calls=%async_computation.1 | async-start | bytes 4718592 | tf_op jit(solution)/shard_map/all_to_all | solution.py:117
  187.6 4.6 copy-start
  187.7 4.6 copy-start.12
  219.1 6.8 copy-start.13
  219.1 7.0 copy-start.14
  219.1 7.2 copy-start.15
  219.1 7.9 copy-start.9
  219.1 71.6 %copy-start.10 = (bf16[192,128]{1,0:T(8,128)(2,1)S(1)}, bf16[192,128]{1,0:T(8,128)(2,1)}, u32[]{:S(2)}) copy-start(bf16[192,128]{1,0:T(8,128)(2,1)} %param.22) | copy-start | bytes 147460
  219.1 154.8 %all-to-all-start = ((bf16[16,24,3072]{2,1,0:T(8,128)(2,1)}), bf16[16,24,3072]{2,1,0:T(8,128)(2,1)}, u32[]{:S(2)}, u32[]{:S(2)}) async-start(bf16[16,24,3072]{2,1,0:T(8,128)(2,1)} %reshape.112), calls=%async_computation | async-start | bytes 4718592 | tf_op jit(solution)/shard_map/all_to_all | solution.py:116
  225.8 887.7 %reduce-scatter.4.cloned.1.call-start = ((), (), s32[]{:S(2)}) async-start(), calls=%async_computation.6 | async-start | bytes 3170304
  317.9 72.8 %copy-start.3 = (bf16[3072,128]{1,0:T(8,128)(2,1)}, bf16[3072,128]{1,0:T(8,128)(2,1)S(1)}, u32[]{:S(2)}) copy-start(bf16[3072,128]{1,0:T(8,128)(2,1)S(1)} %all_gather.23) | copy-start | bytes 2359300
  373.9 4.5 copy-start.8
  377.0 1.5 copy-start.2
  394.0 2.1 copy-start.1
  473.7 1.4 copy-start.6
  473.7 3.2 copy-start.5
Sparse Core Ops, SparseCore 0:
  9.7 93.8 all-gather.5
  105.7 77.2 all-gather.3
  185.4 157.2 all-gather.7
  473.8 639.5 reduce-scatter.3
where the time goes:
time: 1120 us
  waiting for transfers between devices  781 us (70%)
  blocking collectives  207 us (18%)
  local copies, waits for them, and re-layouts  44.2 us (4%)
  matrix products  43.4 us (4%)
  between operations  17.9 us (2%)
  starting transfers between devices  14.8 us (1%)
  other arithmetic  13.3 us (1%)
    unnamed x5, waiting for transfers between devices  634 us
    all_gather x1, waiting for transfers between devices, per_device(): lax.all_gather(projected_values, 'seq', axis=1, tiled=True)  76.4 us
    all_gather x1, waiting for transfers between devices, per_device(): lax.all_gather(projected_keys, 'seq', axis=1, tiled=True)  70.7 us
    all_gather x1, blocking collectives, per_device(): lax.all_gather(adapter_down_weight, 'fsdp', axis=0, tiled=True)  63.7 us
    psum x1, blocking collectives, per_device(): square_total = lax.psum(own_square, ('fsdp', 'seq'))  63.2 us
    unnamed x1, blocking collectives  33.3 us
    all_gather x1, blocking collectives, per_device(): lax.all_gather(adapter_up_weight, 'fsdp', axis=0, tiled=True)  27.3 us
  transfers between devices with their start and end apart: 6, of which 3 were waited for; matrix products, arithmetic and copies ran while one was open for 6% of the time, Pallas kernels for 0%

commit v1 on v0

v1 whole, which is shorter than its diff:
```python
import functools
import math

import jax
import jax.numpy as jnp
from jax import lax
from jax.experimental import pallas as pl
from jax.experimental.pallas import tpu as pltpu
from jax.sharding import PartitionSpec as P

MESH = pl.DeviceIdType.MESH
BF16 = jnp.bfloat16
F32 = jnp.float32

HEAD = 128
ROWS_PER_BLOCK = 8
SAMPLE_STEPS = 16
RANK = 128

adapter_scale = 2.0
adv_floor = 0.5
norm_eps = 1e-06


def noise_levels(timestep):
    level = 1.0 - timestep.astype(jnp.float32) / SAMPLE_STEPS
    return 5.0 * level / (1.0 + 4.0 * level)


def advantages(rewards, group_trajectory_counts):
    count_traj = rewards.shape[0]
    bounds = jnp.cumsum(group_trajectory_counts)
    members = jnp.sum(
        (bounds[None, :] <= jnp.arange(count_traj)[:, None]).astype(jnp.int32), axis=1
    )
    onehot = (members[:, None] == jnp.arange(group_trajectory_counts.shape[0])[None, :]).astype(
        jnp.float32
    )
    counts = jnp.sum(onehot, axis=0)
    group_means = jnp.sum(onehot * rewards[:, None], axis=0) / counts
    spread = rewards - jnp.sum(onehot * group_means[None, :], axis=1)
    variance = jnp.sum(onehot * (spread * spread)[:, None], axis=0) / counts
    deviation = jnp.sum(onehot * jnp.sqrt(variance)[None, :], axis=1)
    return spread / jnp.maximum(deviation, adv_floor)


def enter(groups):
    barrier = pltpu.get_barrier_semaphore()
    total = 0
    for axis, count in groups:
        me = lax.axis_index(axis)
        for offset in range(1, count):
            peer = lax.rem(me + offset, count)
            pl.semaphore_signal(barrier, inc=1, device_id={axis: peer}, device_id_type=MESH)
            total += 1
    pl.semaphore_wait(barrier, total)


def remote(src, dst, send, recv, axis, peer):
    return pltpu.make_async_remote_copy(
        src_ref=src, dst_ref=dst, send_sem=send, recv_sem=recv,
        device_id={axis: peer}, device_id_type=MESH,
    )


def share(axis, count, src, slots, send, recv):
    me = lax.axis_index(axis)
    copies = []
    for offset in range(1, count):
        peer = lax.rem(me + offset, count)
        copy = remote(src, slots.at[me], send.at[offset], recv.at[offset], axis, peer)
        copy.start()
        copies.append(copy)
    slots[me] = src[...]
    return copies


def finish(copies):
    for copy in copies:
        copy.wait()


def attend_kernel(
    n_seq, n_fsdp, q, k, v, hidden, head, final, rewards,
    qa, ka, va, oa, ar, mine, slots, send, recv, local, bsend, brecv,
    s1, r1, s2, r2,
):
    s = lax.axis_index("seq")
    rows = q.shape[0]
    width = q.shape[1] // n_seq
    length = rows * n_seq
    heads = width // HEAD
    enter((("seq", n_seq), ("fsdp", n_fsdp)))

    def cols(i):
        return pl.ds(pl.multiple_of(i * width, 128), width)

    def rws(i):
        return pl.ds(pl.multiple_of(i * rows, 128), rows)

    copies = []
    for j, (src, dst) in enumerate(((k, ka), (q, qa), (v, va))):
        for offset in range(1, n_seq):
            peer = lax.rem(s + offset, n_seq)
            copy = remote(src.at[:, cols(peer)], dst.at[rws(s), :], send.at[j, offset],
                          recv.at[j, offset], "seq", peer)
            copy.start()
            copies.append(copy)
        own = pltpu.make_async_copy(src.at[:, cols(s)], dst.at[rws(s), :], local.at[j])
        own.start()
        copies.append(own)
    finish(copies)

    factor = math.log2(math.e) / math.sqrt(HEAD)
    pairs = n_seq // 2

    def block(j):
        at = pl.ds(pl.multiple_of(j * 2 * rows, 128), 2 * rows)
        for h in range(heads):
            here = slice(h * HEAD, (h + 1) * HEAD)
            scores = lax.dot_general(qa[at, here], ka[:, here], (((1,), (1,)), ((), ())),
                                     preferred_element_type=F32)
            top = jnp.max(scores, axis=1, keepdims=True)
            expo = jnp.exp2((scores - top) * factor)
            total = jnp.sum(expo, axis=1, keepdims=True)
            out = jnp.dot(expo.astype(BF16), va[:, here], preferred_element_type=F32) / total
            oa[at, here] = out.astype(BF16)

    def back(peer):
        offset = lax.rem(peer - s + n_seq, n_seq)
        return remote(oa.at[rws(peer), :], ar.at[:, cols(s)], bsend.at[offset], brecv.at[offset],
                      "seq", peer)

    for i in range(pairs):
        j = lax.rem(s // 2 + 1 + i, pairs)
        block(j)
        if i < pairs - 1:
            for half in range(2):
                back(2 * j + half).start()
        else:
            back(s + 1 - 2 * lax.rem(s, 2)).start()
    ar[:, cols(s)] = oa[rws(s), :]
    for offset in range(1, n_seq):
        back(lax.rem(s + offset, n_seq)).wait()

    reward = jnp.zeros((1, 1), F32)
    for c in range(n_seq):
        here = slice(c * width, (c + 1) * width)
        value = (hidden[:, here].astype(F32) + ar[:, here].astype(F32)).astype(BF16)
        final[:, here] = value
        part = jnp.sum(value.astype(F32) * head[:, here], axis=0, keepdims=True)
        reward = reward + jnp.sum(part, axis=1, keepdims=True)
    mine[...] = jnp.broadcast_to(reward / math.sqrt(length), mine.shape)
    finish(share("seq", n_seq, mine, slots, s1, r1))
    total = slots[0]
    for c in range(1, n_seq):
        total = total + slots[c]
    mine[...] = total
    finish(share("fsdp", n_fsdp, mine, rewards, s2, r2))


def attend(q, k, v, hidden, head, n_seq, n_fsdp):
    rows, features = q.shape
    width = features // n_seq
    vmem = pl.BlockSpec(memory_space=pltpu.VMEM)
    hbm = pl.BlockSpec(memory_space=pl.ANY)
    dma = pltpu.SemaphoreType.DMA
    return pl.pallas_call(
        functools.partial(attend_kernel, n_seq, n_fsdp),
        out_shape=(
            jax.ShapeDtypeStruct((rows, features), BF16),
            jax.ShapeDtypeStruct((n_fsdp, 8, 128), F32),
        ),
        in_specs=[hbm, hbm, hbm, vmem, vmem],
        out_specs=(vmem, vmem),
        scratch_shapes=[
            pltpu.VMEM((rows * n_seq, width), BF16),
            pltpu.VMEM((rows * n_seq, width), BF16),
            pltpu.VMEM((rows * n_seq, width), BF16),
            pltpu.VMEM((rows * n_seq, width), BF16),
            pltpu.VMEM((rows, features), BF16),
            pltpu.VMEM((8, 128), F32),
            pltpu.VMEM((n_seq, 8, 128), F32),
            dma((3, n_seq)), dma((3, n_seq)), dma((3,)),
            dma((n_seq,)), dma((n_seq,)),
            dma((n_seq,)), dma((n_seq,)),
            dma((n_fsdp,)), dma((n_fsdp,)),
        ],
        compiler_params=pltpu.CompilerParams(
            collective_id=0, has_side_effects=True, vmem_limit_bytes=40 * 2**20
        ),
        cost_estimate=pl.CostEstimate(flops=2 * 10**9, bytes_accessed=5 * 2**20, transcendentals=3 * 2**20),
    )(q, k, v, hidden, head)


def grads_kernel(
    n_seq, n_fsdp, noisy, slope, lows, meta, down_out, up_out, loss_out,
    nt, st, na, sa, la, ma, left, sh, mine, slots1, slots2, gt, gslots,
    send, recv, s1, r1, s2, r2, s3, r3,
):
    t = lax.axis_index("fsdp")
    s = lax.axis_index("seq")
    rows, features = noisy.shape
    width = features // n_fsdp
    own = width // n_seq
    enter((("fsdp", n_fsdp), ("seq", n_seq)))

    for c in range(features // 128):
        here = slice(c * 128, (c + 1) * 128)
        nt[here, :] = noisy[:, here].T
        st[here, :] = slope[:, here].T

    def feat(i):
        return pl.ds(pl.multiple_of(i * width, 16), width)

    def toks(i):
        return pl.ds(pl.multiple_of(i * rows, 128), rows)

    copies = []
    for offset in range(1, n_fsdp):
        peer = lax.rem(t + offset, n_fsdp)
        for j, (src, dst) in enumerate((
            (nt.at[feat(peer), :], na.at[:, toks(t)]),
            (st.at[feat(peer), :], sa.at[:, toks(t)]),
            (lows, la.at[:, toks(t)]),
            (meta, ma.at[:, toks(t)]),
        )):
            copy = remote(src, dst, send.at[j, offset], recv.at[j, offset], "fsdp", peer)
            copy.start()
            copies.append(copy)
    na[:, toks(t)] = nt[feat(t), :]
    sa[:, toks(t)] = st[feat(t), :]
    la[:, toks(t)] = lows[...]
    ma[:, toks(t)] = meta[...]
    finish(copies)

    owner = ma[0:1, :]
    loss = ma[1:2, :]
    loss_out[...] = jnp.broadcast_to(
        jnp.sum(jnp.where(owner == t.astype(F32), loss, 0.0), axis=1, keepdims=True), loss_out.shape
    )
    lane = lax.broadcasted_iota(jnp.int32, (8, 128), 1)
    norms = jnp.zeros((8, 128), F32)
    batch = 4
    for g in range(n_fsdp // batch):
        for e in range(batch):
            hot = jnp.where(owner == float(g * batch + e), 1.0, 0.0)
            hot = jnp.broadcast_to(hot, (16, owner.shape[1])).astype(BF16)
            for j in range(2):
                for r in range(RANK // 16):
                    left[j, e * RANK + r * 16:e * RANK + r * 16 + 16, :] = (
                        la[j * RANK + r * 16:j * RANK + r * 16 + 16, :] * hot
                    )
        for j, other in enumerate((na, sa)):
            prod = lax.dot_general(left[j], other[...], (((1,), (1,)), ((), ())),
                                   preferred_element_type=F32)
            if j == 1:
                prod = adapter_scale * prod
            for e in range(batch):
                piece = prod[e * RANK:(e + 1) * RANK]
                d = g * batch + e
                sh[d, j * RANK:(j + 1) * RANK, :] = piece
                square = jnp.sum(jnp.sum(piece * piece, axis=0, keepdims=True), axis=1, keepdims=True)
                norms = jnp.where(lane == d, norms + square, norms)
    mine[...] = norms
    finish(share("fsdp", n_fsdp, mine, slots1, s1, r1))
    norms = slots1[0]
    for c in range(1, n_fsdp):
        norms = norms + slots1[c]
    mine[...] = norms
    finish(share("seq", n_seq, mine, slots2, s2, r2))
    every = slots2[0]
    for c in range(1, n_seq):
        every = every + slots2[c]
    square_total = jnp.sum(every[0:1, :], axis=1, keepdims=True)
    limit = jnp.sqrt(square_total / (n_fsdp * n_seq) + norm_eps)
    clip = limit / jnp.maximum(jnp.sqrt(norms[0:1, :]), limit)
    lane1 = lax.broadcasted_iota(jnp.int32, (1, 128), 1)
    factors = [jnp.sum(jnp.where(lane1 == d, clip, 0.0), axis=1, keepdims=True) for d in range(n_fsdp)]
    for j in range(2):
        here = slice(j * RANK, (j + 1) * RANK)
        total = factors[0] * sh[0, here, :]
        for d in range(1, n_fsdp):
            total = total + factors[d] * sh[d, here, :]
        gt[:, here] = total.T

    copies = []
    for offset in range(1, n_seq):
        peer = lax.rem(s + offset, n_seq)
        copy = remote(gt.at[pl.ds(pl.multiple_of(peer * own, 8), own), :], gslots.at[s],
                      s3.at[offset], r3.at[offset], "seq", peer)
        copy.start()
        copies.append(copy)
    gslots[s] = gt[pl.ds(pl.multiple_of(s * own, 8), own), :]
    finish(copies)
    total = gslots[0]
    for c in range(1, n_seq):
        total = total + gslots[c]
    down_out[...] = total[:, :RANK]
    up_out[...] = total[:, RANK:]


def grads(noisy, slope, lows, meta, n_seq, n_fsdp):
    rows, features = noisy.shape
    width = features // n_fsdp
    own = width // n_seq
    every = rows * n_fsdp
    vmem = pl.BlockSpec(memory_space=pltpu.VMEM)
    dma = pltpu.SemaphoreType.DMA
    return pl.pallas_call(
        functools.partial(grads_kernel, n_seq, n_fsdp),
        out_shape=(
            jax.ShapeDtypeStruct((own, RANK), F32),
            jax.ShapeDtypeStruct((own, RANK), F32),
            jax.ShapeDtypeStruct((8, 128), F32),
        ),
        in_specs=[vmem] * 4,
        out_specs=(vmem,) * 3,
        scratch_shapes=[
            pltpu.VMEM((features, rows), BF16),
            pltpu.VMEM((features, rows), BF16),
            pltpu.VMEM((width, every), BF16),
            pltpu.VMEM((width, every), BF16),
            pltpu.VMEM((2 * RANK, every), BF16),
            pltpu.VMEM((8, every), F32),
            pltpu.VMEM((2, 4 * RANK, every), BF16),
            pltpu.VMEM((n_fsdp, 2 * RANK, width), F32),
            pltpu.VMEM((8, 128), F32),
            pltpu.VMEM((n_fsdp, 8, 128), F32),
            pltpu.VMEM((n_seq, 8, 128), F32),
            pltpu.VMEM((width, 2 * RANK), F32),
            pltpu.VMEM((n_seq, own, 2 * RANK), F32),
            dma((4, n_fsdp)), dma((4, n_fsdp)),
            dma((n_fsdp,)), dma((n_fsdp,)),
            dma((n_seq,)), dma((n_seq,)),
            dma((n_seq,)), dma((n_seq,)),
        ],
        compiler_params=pltpu.CompilerParams(
            collective_id=1, has_side_effects=True, vmem_limit_bytes=40 * 2**20
        ),
        cost_estimate=pl.CostEstimate(flops=4 * 10**9, bytes_accessed=2 * 2**20, transcendentals=0),
    )(noisy, slope, lows, meta)


def per_device(
    incoming_hidden_state, projected_queries, projected_keys, projected_values, training_noise,
    group_trajectory_counts, timestep, block_shard_owner, frozen_weight, adapter_down_weight,
    adapter_up_weight, linear_reward_head,
):
    rows, features = incoming_hidden_state.shape[1:]
    n_seq = lax.axis_size("seq")
    n_fsdp = lax.axis_size("fsdp")
    length = rows * n_seq
    t = lax.axis_index("fsdp")
    frozen = lax.all_gather(frozen_weight, "fsdp", axis=0, tiled=True)
    adapters = lax.all_gather(
        jnp.concatenate([adapter_down_weight, adapter_up_weight], axis=1), "fsdp", axis=0, tiled=True
    )
    down_weight, up_weight = adapters[:, :RANK], adapters[:, RANK:]
    final, slots = attend(
        projected_queries[0], projected_keys[0], projected_values[0], incoming_hidden_state[0],
        linear_reward_head[None, :], n_seq, n_fsdp,
    )
    advantage = advantages(slots[:, 0, 0], group_trajectory_counts)[t]
    level = noise_levels(timestep)[t]
    latent = final.astype(F32)
    fresh = training_noise[0].astype(F32)
    noisy = ((1.0 - level) * latent + level * fresh).astype(BF16)
    target = fresh - latent
    lowrank = jnp.dot(noisy, down_weight, preferred_element_type=F32).astype(BF16)
    error = (
        jnp.dot(noisy, frozen, preferred_element_type=F32)
        + adapter_scale * lax.dot_general(lowrank, up_weight, (((1,), (1,)), ((), ())),
                                          preferred_element_type=F32)
        - target
    )
    token_loss = advantage * jnp.mean(error * error, axis=1) / rows
    slope = (advantage * error / length).astype(BF16)
    back = (adapter_scale * jnp.dot(slope, up_weight, preferred_element_type=F32)).astype(BF16)
    lows = jnp.concatenate([back.T, lowrank.T], axis=0)
    owners = jnp.repeat(block_shard_owner[0, :, 0], ROWS_PER_BLOCK).astype(F32)
    meta = jnp.concatenate([owners[None], token_loss[None], jnp.zeros((6, rows), F32)], axis=0)
    grad_down, grad_up, loss = grads(noisy, slope, lows, meta, n_seq, n_fsdp)
    return final[None], grad_down, grad_up, loss[:1, :1]


def solution(mesh):
    return jax.shard_map(
        per_device,
        mesh=mesh,
        in_specs=(
            P("fsdp", "seq", None),
            P("fsdp", "seq", None),
            P("fsdp", "seq", None),
            P("fsdp", "seq", None),
            P("fsdp", "seq", None),
            P(),
            P(),
            P("fsdp", "seq", None),
            P("fsdp", None),
            P("fsdp", None),
            P("fsdp", None),
            P(),
        ),
        out_specs=(
            P("fsdp", "seq", None),
            P(("fsdp", "seq"), None),
            P(("fsdp", "seq"), None),
            P("fsdp", "seq"),
        ),
        check_vma=False,
    )
```

time: 1120 us -> 288 us (0.26)
  waiting for transfers between devices: 781 us -> 116 us
  blocking collectives: 207 us -> 0 us
  Pallas kernels: 0 us -> 132 us
  local copies, waits for them, and re-layouts: 44.2 us -> 9.47 us
  matrix products: 43.4 us -> 11.5 us
  starting transfers between devices: 14.8 us -> 0.08 us
    unnamed x5 -> x2, waiting for transfers between devices: 634 us -> 0.71 us
    pallas_call x0 -> x2, Pallas kernels: none -> 132 us  [the longest x1 71 us: grads(): pl.pallas_call(functools.partial(grads_kernel, n_seq, n_fsdp), out_shape=...]
    all_gather x2 -> x0, blocking collectives: 91 us -> none  [the longest x1 63.7 us: per_device(): lax.all_gather(adapter_down_weight, 'fsdp', axis=0, tiled=True)]
    psum x2 -> x0, blocking collectives: 83.1 us -> none  [the longest x1 63.2 us: per_device(): square_total = lax.psum(own_square, ('fsdp', 'seq'))]
    unnamed x1 -> x0, blocking collectives: 33.3 us -> none
    dot_general x9 -> x4, matrix products: 43.4 us -> 11.5 us  [the longest x1 8.08 us: per_device(): jnp.dot(noisy, frozen, preferred_element_type=F32)]
    all_gather x3 -> x2, waiting for transfers between devices: 147 us -> 116 us  [the longest x1 116 us: per_device(): frozen = lax.all_gather(frozen_weight, 'fsdp', axis=0, tiled=True)]
    all_to_all x2 -> x0, starting transfers between devices: 14.6 us -> none  [the longest x1 7.93 us: per_device(): lax.all_to_all(place(training_noise[0]), 'fsdp', split_axis=0, concat_axi...]
  transfers between devices with their start and end apart: 6 -> 2, of which waited for: 3 -> 1; matrix products, arithmetic and copies ran while one was open for 6% -> 2% of each run, Pallas kernels for 0% -> 21%
where the time goes in v1:
time: 288 us
  Pallas kernels  132 us (46%)
  waiting for transfers between devices  116 us (40%)
  between operations  15.5 us (5%)
  matrix products  11.5 us (4%)
  local copies, waits for them, and re-layouts  9.47 us (3%)
  other arithmetic  3.23 us (1%)
    all_gather x1, waiting for transfers between devices, per_device(): frozen = lax.all_gather(frozen_weight, 'fsdp', axis=0, tiled=True)  116 us
    pallas_call x1, Pallas kernels, grads(): pl.pallas_call(functools.partial(grads_kernel, n_seq, n_fsdp), out_shape=...  71 us
    pallas_call x1, Pallas kernels, attend(): pl.pallas_call(functools.partial(attend_kernel, n_seq, n_fsdp), out_shape...  60.9 us
    dot_general x1, matrix products, per_device(): jnp.dot(noisy, frozen, preferred_element_type=F32)  8.08 us
    unnamed x23, local copies, waits for them, and re-layouts  7.33 us
  transfers between devices with their start and end apart: 2, of which 1 were waited for; matrix products, arithmetic and copies ran while one was open for 2% of the time, Pallas kernels for 21%

profile of v1, /device:TPU:0, one launch (start us, length us, event | category | flops | bytes accessed | tf_op | source)
XLA Modules:
  0.0 288.0 jit_solution(11219026067591824866)
XLA Ops:
  7.2 0.0 all-gather.5.cloned.1.call-start
  7.2 1.5 pad_maximum_fusion
  8.7 0.0 all-gather.5.cloned.1.call-update
  8.7 0.0 all-gather.3.cloned.1.call-start
  8.8 0.7 all-gather.3.cloned.1.call-update
  9.5 0.0 copy-start
  9.5 1.1 copy-done
  10.6 0.0 copy-start.1
  10.6 1.1 copy-done.1
  11.7 0.0 copy-start.2
  11.7 1.1 copy-done.2
  12.9 0.0 copy-start.3
  12.9 1.1 copy-done.3
  14.0 0.0 copy-start.4
  14.0 0.7 copy-done.4
  14.7 0.0 copy-start.7
  14.7 0.0 copy-start.9
  14.7 60.9 %shard_map.147 = (bf16[128,3072]{1,0:T(8,128)(2,1)S(1)}, f32[16,8,128]{2,1,0:T(8,128)S(1)}) custom-call(bf16[128,3072]{1,0:T(8,128)(2,1)S(1)} %bitcast.25, bf16[128,3072]{1,0:T(8,128)(2,1)S(1)} %bitcast.26, bf16[128,3072]{1,0:T(8,128)(2,1)S(1)} %bitcast.27, bf16[128,3072]{1,0:T(8,128)(2,1)S(1)} %bitcast.28, f32[1,3072]{1,0:T(1,128)S(1)} %bitcast.29), custom_call_target="tpu_custom_call" | custom-call | flops 2000000000 | bytes 5242880 | tf_op jit(solution)/shard_map/pallas_call | solution.py:168
  75.6 0.0 copy-done.7
  75.6 0.2 reduce-window.8
  75.8 0.0 copy-done.8
  75.8 0.6 dynamic_slice.6
  76.4 0.1 convert_reduce_fusion.1
  76.5 0.2 slice_reduce_fusion
  76.7 0.1 convert_reduce_fusion
  76.8 0.1 select_reduce_fusion.2
  76.9 0.1 select_reduce_fusion.1
  77.1 0.1 select_reduce_fusion
  77.2 0.6 dynamic_slice.7
  77.8 0.0 copy-done.9
  77.8 0.1 broadcast_in_dim.10
  77.8 0.1 convert_element_type.65
  79.2 0.1 pad.2.clone
  79.3 0.0 copy-done.5
  79.3 0.9 fusion.3.noisy
  80.3 0.0 all-gather.5.cloned.1.call-done
  80.3 1.6 convolution_convert_fusion
  81.9 115.6 %all-gather.3.cloned.1.call-done = bf16[3072,3072]{1,0:T(8,128)(2,1)} async-done(((bf16[192,3072]{1,0:T(8,128)(2,1)}), bf16[3072,3072]{1,0:T(8,128)(2,1)}) %all-gather.3.cloned.1.call-update) | async-done | bytes 18874384 | tf_op jit(solution)/shard_map/all_gather | solution.py:355
  197.5 8.1 %fusion.9 = f32[128,3072]{1,0:T(8,128)S(1)} fusion(bf16[128,3072]{1,0:T(8,128)(2,1)S(1)} %fusion.3.noisy, bf16[3072,3072]{1,0:T(8,128)(2,1)} %all-gather.3.cloned.1.call-done), kind=kOutput, calls=%fused_computation.34 | convolution fusion | flops 2415919104 | bytes 21233664 | tf_op jit(solution)/shard_map/dot_general | solution.py:372
  205.6 0.0 copy-done.6
  205.6 1.5 multiply_reduce_fusion
  207.0 0.4 fusion.4
  207.5 0.1 maximum_maximum_fusion.meta
  207.6 71.0 %shard_map.148 = (f32[24,128]{1,0:T(8,128)S(1)}, f32[24,128]{1,0:T(8,128)S(1)}, f32[8,128]{1,0:T(8,128)S(1)}) custom-call(bf16[128,3072]{1,0:T(8,128)(2,1)S(1)} %fusion.3.noisy, bf16[128,3072]{1,0:T(8,128)(2,1)S(1)} %get-tuple-element.19.slope, bf16[256,128]{1,0:T(8,128)(2,1)S(1)} %pad_maximum_fusion.1.lows, f32[8,128]{1,0:T(8,128)S(1)} %maximum_maximum_fusion.meta), custom_call_target="tpu_custom_call" | custom-call | flops 4000000000 | bytes 2097152 | tf_op jit(solution)/shard_map/pallas_call | solution.py:310
  278.6 0.5 slice.15
  279.1 0.9 copy.19
  280.0 0.6 copy.20
  280.6 0.6 copy.21
  (12 shorter events, 0.1 us)
Async XLA Ops:
  7.2 73.1 %all-gather.5.cloned.1.call-start = ((), (), s32[]{:S(2)}) async-start(), calls=%async_computation.1 | async-start | bytes 1671168 | tf_op jit(solution)/shard_map/all_gather | solution.py:356
  8.7 188.8 %all-gather.3.cloned.1.call-start = ((), (), s32[]{:S(2)}) async-start(), calls=%async_computation | async-start | bytes 20054016 | tf_op jit(solution)/shard_map/all_gather | solution.py:355
  9.5 1.1 copy-start
  10.6 1.1 copy-start.1
  11.7 1.1 copy-start.2
  12.9 1.1 copy-start.3
  14.0 0.7 copy-start.4
  14.7 60.9 %copy-start.7 = (s32[4]{0:T(128)S(1)}, s32[4]{0:T(128)}, u32[]{:S(2)}) copy-start(s32[4]{0:T(128)} %param.17) | copy-start | bytes 52
  14.7 61.1 %copy-start.8 = (s32[16]{0:T(128)S(1)}, s32[16]{0:T(128)}, u32[]{:S(2)}) copy-start(s32[16]{0:T(128)} %param.18) | copy-start | bytes 196
  14.7 63.0 %copy-start.9 = (s32[1,16,1]{1,2,0:T(1,128)S(1)}, s32[1,16,1]{1,2,0:T(1,128)}, u32[]{:S(2)}) copy-start(s32[1,16,1]{1,2,0:T(1,128)} %param.19) | copy-start | bytes 196
  14.7 64.6 %copy-start.5 = (bf16[1,128,3072]{2,1,0:T(8,128)(2,1)S(1)}, bf16[1,128,3072]{2,1,0:T(8,128)(2,1)}, u32[]{:S(2)}) copy-start(bf16[1,128,3072]{2,1,0:T(8,128)(2,1)} %param.16) | copy-start | bytes 2359300
  197.5 8.1 %copy-start.6 = (bf16[3072,256]{1,0:T(8,128)(2,1)S(1)}, bf16[3072,256]{1,0:T(8,128)(2,1)}, u32[]{:S(2)}) copy-start(bf16[3072,256]{1,0:T(8,128)(2,1)} %all-gather.5.cloned.1.call-done) | copy-start | bytes 4718596
Sparse Core Ops, SparseCore 0:
  11.0 64.5 all-gather.4
  78.0 119.4 all-gather.2

commit v2 on v1

v2 whole, which is shorter than its diff:
```python
import functools
import math

import jax
import jax.numpy as jnp
from jax import lax
from jax.experimental import pallas as pl
from jax.experimental.pallas import tpu as pltpu
from jax.sharding import PartitionSpec as P

MESH = pl.DeviceIdType.MESH
BF16 = jnp.bfloat16
F32 = jnp.float32

HEAD = 128
ROWS_PER_BLOCK = 8
SAMPLE_STEPS = 16
RANK = 128
SPLIT = 1792

adapter_scale = 2.0
adv_floor = 0.5
norm_eps = 1e-06


def remote(src, dst, send, recv, axis, peer):
    return pltpu.make_async_remote_copy(
        src_ref=src, dst_ref=dst, send_sem=send, recv_sem=recv,
        device_id={axis: peer}, device_id_type=MESH,
    )


def share(axis, count, src, slots, send, recv):
    me = lax.axis_index(axis)
    copies = []
    for offset in range(1, count):
        peer = lax.rem(me + offset, count)
        copy = remote(src, slots.at[me], send.at[offset], recv.at[offset], axis, peer)
        copy.start()
        copies.append(copy)
    slots[me] = src[...]
    return copies


def finish(copies):
    for copy in copies:
        copy.wait()


def advantage_row(counts, rewards, lane):
    result = jnp.zeros_like(rewards)
    low = jnp.int32(0)
    for g in range(counts.shape[0]):
        high = low + counts[g]
        inside = jnp.where((lane >= low) & (lane < high), 1.0, 0.0)
        number = jnp.sum(inside, axis=1, keepdims=True)
        mean = jnp.sum(inside * rewards, axis=1, keepdims=True) / number
        dev = inside * (rewards - mean)
        spread = jnp.sqrt(jnp.sum(dev * dev, axis=1, keepdims=True) / number)
        result = result + dev / jnp.maximum(spread, adv_floor)
        low = high
    return result


def step_kernel(
    n_seq, n_fsdp,
    hidden_in, q, k, v, noise_in, counts, steps, owners, frozen, down, up, head,
    final, down_out, up_out, loss_out,
    hidden, noise, wb, qa, ka, va, oa, ar, noisy, acc, nt, st, na, sa, la, ma, left, sh,
    mine, meta, lows, rslots, rewards, slots1, slots2, gt, gslots,
    ksend, krecv, klocal, wsend, wrecv, bsend, brecv, r1s, r1r, r2s, r2r,
    send, recv, s1, r1, s2, r2, s3, r3,
):
    t = lax.axis_index("fsdp")
    s = lax.axis_index("seq")
    rows, features = q.shape
    width = features // n_seq
    length = rows * n_seq
    heads = width // HEAD
    nr = frozen.shape[0]
    nc = wb.shape[1]
    own = nr // n_seq
    x, zh, core = t // 4, lax.rem(t // 2, 2), lax.rem(t, 2)
    xp, xm, xo, zz = lax.rem(x + 1, 4), lax.rem(x + 3, 4), lax.rem(x + 2, 4), 1 - zh

    def place(a, b):
        return a * 4 + b * 2 + core

    dev_xp, dev_xm = (place(xp, zh), s), (place(xm, zh), s)
    dev_z = (place(x, zz), lax.rem(s + n_seq // 2, n_seq))
    dev_core = (x * 4 + zh * 2 + 1 - core, s)

    barrier = pltpu.get_barrier_semaphore()
    for axis, count, me in (("seq", n_seq, s), ("fsdp", n_fsdp, t)):
        for offset in range(1, count):
            pl.semaphore_signal(barrier, inc=1, device_id={axis: lax.rem(me + offset, count)},
                                device_id_type=MESH)
    pl.semaphore_signal(barrier, inc=1, device_id=dev_z, device_id_type=MESH)

    def span(i, size):
        return pl.ds(pl.multiple_of(i * size, 128), size)

    def feat(i):
        return pl.ds(pl.multiple_of(i * nr, 16), nr)

    wlocal = []
    for j, (part, at, size) in enumerate(((frozen, 0, features), (down, features, RANK),
                                          (up, features + RANK, RANK))):
        wlocal.append(pltpu.make_async_copy(part, wb.at[feat(t), pl.ds(at, size)], klocal.at[j]))
    klocals = []
    for j, (part, dst) in enumerate(((k, ka), (q, qa), (v, va))):
        klocals.append(pltpu.make_async_copy(part.at[:, span(s, width)], dst.at[span(s, rows), :],
                                             klocal.at[3 + j]))
    hlocal = [pltpu.make_async_copy(hidden_in, hidden, klocal.at[6]),
              pltpu.make_async_copy(noise_in, noise, klocal.at[7])]
    for copy in wlocal + klocals + hlocal:
        copy.start()
    pl.semaphore_wait(barrier, n_seq + n_fsdp - 1)

    kcopies = []

    def scatter(j, part, dst):
        for offset in range(1, n_seq):
            peer = lax.rem(s + offset, n_seq)
            copy = remote(part.at[:, span(peer, width)], dst.at[span(s, rows), :],
                          ksend.at[j, offset], krecv.at[j, offset], "seq", peer)
            copy.start()
            kcopies.append(copy)

    half = nr // 2
    whole, first, second = (0, nr), (0, half), (half, half)
    every, near, far = (0, nc), (0, SPLIT), (SPLIT, nc - SPLIT)
    wcopies = {}

    def pass_on(i, block, part, columns, device):
        ref = wb.at[pl.ds(pl.multiple_of(block * nr + part[0], 16), part[1]),
                    pl.ds(columns[0], columns[1])]
        wcopies[i] = pltpu.make_async_remote_copy(
            src_ref=ref, dst_ref=ref, send_sem=wsend.at[i], recv_sem=wrecv.at[i],
            device_id=device, device_id_type=MESH)
        wcopies[i].start()

    def arrived(*which):
        for i in which:
            wcopies[i].wait_recv()

    scatter(0, k, ka)
    finish(wlocal)
    pass_on(0, t, whole, every, dev_xp)
    pass_on(1, t, whole, every, dev_xm)
    pass_on(2, t, whole, every, dev_z)
    pass_on(3, t, whole, every, dev_core)
    scatter(1, q, qa)
    scatter(2, v, va)

    arrived(0, 1, 2)
    pass_on(4, place(xm, zh), first, every, dev_xp)
    pass_on(5, place(xp, zh), second, every, dev_xm)
    pass_on(8, place(xm, zh), whole, far, dev_z)
    pass_on(9, place(xp, zh), whole, far, dev_z)
    pass_on(6, place(x, zz), whole, near, dev_xp)
    pass_on(7, place(x, zz), whole, near, dev_xm)
    pass_on(10, place(xm, zh), whole, every, dev_core)
    pass_on(11, place(xp, zh), whole, every, dev_core)
    pass_on(12, place(x, zz), whole, every, dev_core)

    finish(klocals + kcopies)
    factor = math.log2(math.e) / math.sqrt(HEAD)
    pairs = n_seq // 2

    def back_copy(peer):
        offset = lax.rem(peer - s + n_seq, n_seq)
        return remote(oa.at[span(peer, rows), :], ar.at[:, span(s, width)], bsend.at[offset],
                      brecv.at[offset], "seq", peer)

    for i in range(pairs):
        j = lax.rem(s // 2 + 1 + i, pairs)
        at = span(j, 2 * rows)
        for h in range(heads):
            here = slice(h * HEAD, (h + 1) * HEAD)
            scores = lax.dot_general(qa[at, here], ka[:, here], (((1,), (1,)), ((), ())),
                                     preferred_element_type=F32)
            top = jnp.max(scores, axis=1, keepdims=True)
            expo = jnp.exp2((scores - top) * factor)
            total = jnp.sum(expo, axis=1, keepdims=True)
            out = jnp.dot(expo.astype(BF16), va[:, here], preferred_element_type=F32) / total
            oa[at, here] = out.astype(BF16)
        if i < pairs - 1:
            for part in range(2):
                back_copy(2 * j + part).start()
        else:
            back_copy(s + 1 - 2 * lax.rem(s, 2)).start()
    ar[:, span(s, width)] = oa[span(s, rows), :]

    arrived(4, 5)
    pass_on(13, place(xo, zh), whole, far, dev_z)
    pass_on(14, place(xo, zh), whole, every, dev_core)

    finish(hlocal)
    for offset in range(1, n_seq):
        back_copy(lax.rem(s + offset, n_seq)).wait()
    step = jnp.full((1, 1), steps[t], jnp.int32).astype(F32)
    level = 1.0 - step / SAMPLE_STEPS
    level = 5.0 * level / (1.0 + 4.0 * level)
    reward = jnp.zeros((1, 1), F32)
    for c in range(n_seq):
        here = slice(c * width, (c + 1) * width)
        value = (hidden[:, here].astype(F32) + ar[:, here].astype(F32)).astype(BF16)
        final[:, here] = value
        value = value.astype(F32)
        part = jnp.sum(value * head[:, here], axis=0, keepdims=True)
        reward = reward + jnp.sum(part, axis=1, keepdims=True)
        noised = ((1.0 - level) * value + level * noise[:, here].astype(F32)).astype(BF16)
        noisy[:, here] = noised
        nt[here, :] = noised.T
    mine[...] = jnp.broadcast_to(reward / math.sqrt(length), mine.shape)
    rcopies = share("seq", n_seq, mine, rslots, r1s, r1r)

    def slices(j, part, dst, peer):
        offset = lax.rem(peer - t + n_fsdp, n_fsdp)
        return remote(part.at[feat(peer), :], dst.at[:, span(t, rows)], send.at[j, offset],
                      recv.at[j, offset], "fsdp", peer)

    def spread(j, part, dst):
        copies = []
        for offset in range(1, n_fsdp):
            peer = lax.rem(t + offset, n_fsdp)
            copy = remote(part, dst, send.at[j, offset], recv.at[j, offset], "fsdp", peer)
            copy.start()
            copies.append(copy)
        return copies

    for offset in range(1, n_fsdp):
        slices(0, nt, na, lax.rem(t + offset, n_fsdp)).start()
    na[:, span(t, rows)] = nt[feat(t), :]

    tile = (features + RANK) // 5

    def multiply(a, b, start=False):
        here = span(a * 2 + b, 2 * nr)
        for c in range(5):
            cols = slice(c * tile, (c + 1) * tile)
            part = jnp.dot(noisy[:, here], wb[here, cols], preferred_element_type=F32)
            acc[:, cols] = part if start else acc[:, cols] + part

    arrived(3)
    multiply(x, zh, True)
    arrived(6, 7)
    pass_on(15, place(xm, zz), first, near, dev_xp)
    pass_on(16, place(xp, zz), second, near, dev_xm)
    pass_on(17, place(xm, zz), whole, near, dev_core)
    pass_on(18, place(xp, zz), whole, near, dev_core)
    finish(rcopies)
    total = rslots[0]
    for c in range(1, n_seq):
        total = total + rslots[c]
    mine[...] = total
    rcopies = share("fsdp", n_fsdp, mine, rewards, r2s, r2r)
    arrived(10)
    multiply(xm, zh)
    arrived(11)
    multiply(xp, zh)
    arrived(8, 9)
    pass_on(19, place(xm, zz), whole, far, dev_core)
    pass_on(20, place(xp, zz), whole, far, dev_core)
    arrived(12)
    multiply(x, zz)
    arrived(14)
    multiply(xo, zh)
    arrived(13, 15, 16)
    pass_on(21, place(xo, zz), whole, every, dev_core)
    arrived(17, 19)
    multiply(xm, zz)
    arrived(18, 20)
    multiply(xp, zz)
    finish(rcopies)
    lane = lax.broadcasted_iota(jnp.int32, (1, 128), 1)
    reward = jnp.zeros((1, 128), F32)
    for c in range(n_fsdp):
        reward = jnp.where(lane == c, rewards[c, 0:1, :], reward)
    advantage = advantage_row(counts, reward, lane)
    advantage = jnp.sum(jnp.where(lane == t, advantage, 0.0), axis=1, keepdims=True)
    arrived(21)
    multiply(xo, zz)

    lowrank = acc[:, features:].astype(BF16)
    lows[1] = lowrank.T
    low_copies = spread(2, lows.at[1], la.at[1, :, span(t, rows)])
    la[1, :, span(t, rows)] = lows[1]
    loss = jnp.zeros((rows, 1), F32)
    back = jnp.zeros((rows, RANK), F32)
    chips = n_fsdp // 2
    for i in range(chips):
        j = lax.rem(t // 2 + 1 + i, chips)
        here = span(j, 2 * nr)
        up_rows = wb[here, features + RANK:]
        target = noise[:, here].astype(F32) - final[:, here].astype(F32)
        error = acc[:, here] + adapter_scale * lax.dot_general(
            lowrank, up_rows, (((1,), (1,)), ((), ())), preferred_element_type=F32) - target
        loss = loss + jnp.sum(error * error, axis=1, keepdims=True)
        slope = (advantage * error / length).astype(BF16)
        st[here, :] = slope.T
        if i < chips - 1:
            for part in range(2):
                slices(1, st, sa, 2 * j + part).start()
        else:
            slices(1, st, sa, t + 1 - 2 * core).start()
        back = back + jnp.dot(slope, up_rows, preferred_element_type=F32)
    sa[:, span(t, rows)] = st[feat(t), :]
    lows[0] = (adapter_scale * back).astype(BF16).T
    low_copies += spread(3, lows.at[0], la.at[0, :, span(t, rows)])
    la[0, :, span(t, rows)] = lows[0]
    token_loss = jnp.broadcast_to(advantage * loss / (features * rows), (rows, 128)).T
    sub = lax.broadcasted_iota(jnp.int32, (8, rows), 0)
    meta[...] = jnp.where(sub == 0, owners[...], token_loss[0:8, :])
    low_copies += spread(4, meta, ma.at[:, span(t, rows)])
    ma[:, span(t, rows)] = meta[...]

    lanes = lax.broadcasted_iota(jnp.int32, (8, 128), 1)
    batch = 4
    norms = jnp.zeros((8, 128), F32)
    finish(low_copies)
    for offset in range(1, n_fsdp):
        slices(0, nt, na, lax.rem(t + offset, n_fsdp)).wait()
        slices(1, st, sa, lax.rem(t + offset, n_fsdp)).wait()
    owner = ma[0:1, :]
    loss_out[...] = jnp.broadcast_to(
        jnp.sum(jnp.where(owner == t.astype(F32), ma[1:2, :], 0.0), axis=1, keepdims=True),
        loss_out.shape)
    for j, other in ((1, sa), (0, na)):
        for g in range(n_fsdp // batch):
            for e in range(batch):
                hot = jnp.where(owner == float(g * batch + e), 1.0, 0.0)
                hot = jnp.broadcast_to(hot, (16, owner.shape[1])).astype(BF16)
                for r in range(RANK // 16):
                    left[j, e * RANK + r * 16:e * RANK + r * 16 + 16, :] = (
                        la[j, r * 16:r * 16 + 16, :] * hot)
            prod = lax.dot_general(left[j], other[...], (((1,), (1,)), ((), ())),
                                   preferred_element_type=F32)
            if j == 1:
                prod = adapter_scale * prod
            for e in range(batch):
                piece = prod[e * RANK:(e + 1) * RANK]
                d = g * batch + e
                sh[d, j * RANK:(j + 1) * RANK, :] = piece
                square = jnp.sum(jnp.sum(piece * piece, axis=0, keepdims=True), axis=1, keepdims=True)
                norms = jnp.where(lanes == d, norms + square, norms)

    mine[...] = norms
    finish(share("fsdp", n_fsdp, mine, slots1, s1, r1))
    norms = slots1[0]
    for c in range(1, n_fsdp):
        norms = norms + slots1[c]
    mine[...] = norms
    finish(share("seq", n_seq, mine, slots2, s2, r2))
    total = slots2[0]
    for c in range(1, n_seq):
        total = total + slots2[c]
    square_total = jnp.sum(total[0:1, :], axis=1, keepdims=True)
    limit = jnp.sqrt(square_total / (n_fsdp * n_seq) + norm_eps)
    clip = limit / jnp.maximum(jnp.sqrt(norms[0:1, :]), limit)
    factors = [jnp.sum(jnp.where(lane == d, clip, 0.0), axis=1, keepdims=True) for d in range(n_fsdp)]
    for j in range(2):
        here = slice(j * RANK, (j + 1) * RANK)
        total = factors[0] * sh[0, here, :]
        for d in range(1, n_fsdp):
            total = total + factors[d] * sh[d, here, :]
        gt[:, here] = total.T

    copies = []
    for offset in range(1, n_seq):
        peer = lax.rem(s + offset, n_seq)
        copy = remote(gt.at[pl.ds(pl.multiple_of(peer * own, 8), own), :], gslots.at[s],
                      s3.at[offset], r3.at[offset], "seq", peer)
        copy.start()
        copies.append(copy)
    gslots[s] = gt[pl.ds(pl.multiple_of(s * own, 8), own), :]
    finish(copies)
    total = gslots[0]
    for c in range(1, n_seq):
        total = total + gslots[c]
    down_out[...] = total[:, :RANK]
    up_out[...] = total[:, RANK:]
    for i in range(len(wcopies)):
        wcopies[i].wait_send()


def per_device(
    incoming_hidden_state, projected_queries, projected_keys, projected_values, training_noise,
    group_trajectory_counts, timestep, block_shard_owner, frozen_weight, adapter_down_weight,
    adapter_up_weight, linear_reward_head,
):
    rows, features = incoming_hidden_state.shape[1:]
    n_seq = lax.axis_size("seq")
    n_fsdp = lax.axis_size("fsdp")
    width = features // n_seq
    part = features // n_fsdp
    own = part // n_seq
    length = rows * n_seq
    every = rows * n_fsdp
    owners = jnp.repeat(block_shard_owner[0, :, 0], ROWS_PER_BLOCK).astype(F32)[None, :]
    vmem = pl.BlockSpec(memory_space=pltpu.VMEM)
    smem = pl.BlockSpec(memory_space=pltpu.SMEM)
    hbm = pl.BlockSpec(memory_space=pl.ANY)
    dma = pltpu.SemaphoreType.DMA
    final, grad_down, grad_up, loss = pl.pallas_call(
        functools.partial(step_kernel, n_seq, n_fsdp),
        out_shape=(
            jax.ShapeDtypeStruct((rows, features), BF16),
            jax.ShapeDtypeStruct((own, RANK), F32),
            jax.ShapeDtypeStruct((own, RANK), F32),
            jax.ShapeDtypeStruct((8, 128), F32),
        ),
        in_specs=[hbm, hbm, hbm, hbm, hbm, smem, smem, vmem, hbm, hbm, hbm, vmem],
        out_specs=(vmem,) * 4,
        scratch_shapes=[
            pltpu.VMEM((rows, features), BF16),
            pltpu.VMEM((rows, features), BF16),
            pltpu.VMEM((features, features + 2 * RANK), BF16),
            pltpu.VMEM((length, width), BF16),
            pltpu.VMEM((length, width), BF16),
            pltpu.VMEM((length, width), BF16),
            pltpu.VMEM((length, width), BF16),
            pltpu.VMEM((rows, features), BF16),
            pltpu.VMEM((rows, features), BF16),
            pltpu.VMEM((rows, features + RANK), F32),
            pltpu.VMEM((features, rows), BF16),
            pltpu.VMEM((features, rows), BF16),
            pltpu.VMEM((part, every), BF16),
            pltpu.VMEM((part, every), BF16),
            pltpu.VMEM((2, RANK, every), BF16),
            pltpu.VMEM((8, every), F32),
            pltpu.VMEM((2, 4 * RANK, every), BF16),
            pltpu.VMEM((n_fsdp, 2 * RANK, part), F32),
            pltpu.VMEM((8, 128), F32),
            pltpu.VMEM((8, rows), F32),
            pltpu.VMEM((2, RANK, rows), BF16),
            pltpu.VMEM((n_seq, 8, 128), F32),
            pltpu.VMEM((n_fsdp, 8, 128), F32),
            pltpu.VMEM((n_fsdp, 8, 128), F32),
            pltpu.VMEM((n_seq, 8, 128), F32),
            pltpu.VMEM((part, 2 * RANK), F32),
            pltpu.VMEM((n_seq, own, 2 * RANK), F32),
            dma((3, n_seq)), dma((3, n_seq)), dma((8,)),
            dma((22,)), dma((22,)),
            dma((n_seq,)), dma((n_seq,)),
            dma((n_seq,)), dma((n_seq,)),
            dma((n_fsdp,)), dma((n_fsdp,)),
            dma((5, n_fsdp)), dma((5, n_fsdp)),
            dma((n_fsdp,)), dma((n_fsdp,)),
            dma((n_seq,)), dma((n_seq,)),
            dma((n_seq,)), dma((n_seq,)),
        ],
        compiler_params=pltpu.CompilerParams(
            collective_id=0, has_side_effects=True, vmem_limit_bytes=58 * 2**20
        ),
        cost_estimate=pl.CostEstimate(
            flops=10**10, bytes_accessed=8 * 2**20, transcendentals=3 * 2**20
        ),
    )(
        incoming_hidden_state[0], projected_queries[0], projected_keys[0], projected_values[0],
        training_noise[0], group_trajectory_counts, timestep, owners, frozen_weight,
        adapter_down_weight, adapter_up_weight, linear_reward_head[None, :],
    )
    return final[None], grad_down, grad_up, loss[:1, :1]


def solution(mesh):
    return jax.shard_map(
        per_device,
        mesh=mesh,
        in_specs=(
            P("fsdp", "seq", None),
            P("fsdp", "seq", None),
            P("fsdp", "seq", None),
            P("fsdp", "seq", None),
            P("fsdp", "seq", None),
            P(),
            P(),
            P("fsdp", "seq", None),
            P("fsdp", None),
            P("fsdp", None),
            P("fsdp", None),
            P(),
        ),
        out_specs=(
            P("fsdp", "seq", None),
            P(("fsdp", "seq"), None),
            P(("fsdp", "seq"), None),
            P("fsdp", "seq"),
        ),
        check_vma=False,
    )
```

time: 288 us -> 144 us (0.50)
  waiting for transfers between devices: 116 us -> 0 us
  between operations: 15.5 us -> 0.66 us
  matrix products: 11.5 us -> 0 us
  Pallas kernels: 132 us -> 138 us
  local copies, waits for them, and re-layouts: 9.47 us -> 5.15 us
    all_gather x2 -> x0, waiting for transfers between devices: 116 us -> none  [the longest x1 116 us: per_device(): frozen = lax.all_gather(frozen_weight, 'fsdp', axis=0, tiled=True)]
    dot_general x4 -> x0, matrix products: 11.5 us -> none  [the longest x1 8.08 us: per_device(): jnp.dot(noisy, frozen, preferred_element_type=F32)]
    pallas_call x2 -> x1, Pallas kernels: 132 us -> 138 us  [per_device(): pl.pallas_call(functools.partial(step_kernel, n_seq, n_fsdp), out_shape=(...]
    unnamed x23 -> x7, local copies, waits for them, and re-layouts: 7.33 us -> 3.27 us
  transfers between devices with their start and end apart: 2 -> 0, of which waited for: 1 -> 0; matrix products, arithmetic and copies ran while one was open for 2% -> 0% of each run, Pallas kernels for 21% -> 0%
where the time goes in v2:
time: 144 us
  Pallas kernels  138 us (96%)
  local copies, waits for them, and re-layouts  5.15 us (4%)
    pallas_call x1, Pallas kernels, per_device(): pl.pallas_call(functools.partial(step_kernel, n_seq, n_fsdp), out_shape=(...  138 us
    unnamed x7, local copies, waits for them, and re-layouts  3.27 us

profile of v2, /device:TPU:0, one launch (start us, length us, event | category | flops | bytes accessed | tf_op | source)
XLA Modules:
  0.0 144.1 jit_solution(8362577151686780914)
XLA Ops:
  0.6 0.7 convert_bitcast_fusion
  1.3 0.1 broadcast_in_dim.10
  1.4 0.6 convert_element_type.19.owners
  2.0 137.6 %shard_map.147 = (bf16[128,3072]{1,0:T(8,128)(2,1)}, f32[24,128]{1,0:T(8,128)}, f32[24,128]{1,0:T(8,128)}, f32[8,128]{1,0:T(8,128)}) custom-call(bf16[128,3072]{1,0:T(8,128)(2,1)} %bitcast.10, bf16[128,3072]{1,0:T(8,128)(2,1)} %bitcast.11, bf16[128,3072]{1,0:T(8,128)(2,1)} %bitcast.12, bf16[128,3072]{1,0:T(8,128)(2,1)} %bitcast.13, ...), custom_call_target="tpu_custom_call" | custom-call | flops 10000000000 | bytes 8388608 | tf_op jit(solution)/shard_map/pallas_call | solution.py:406
  139.6 0.0 copy-start.1
  139.6 0.0 copy-start
  139.6 1.2 slice.3
  140.8 2.1 %copy.19 = bf16[1,128,3072]{2,1,0:T(8,128)(2,1)} copy(bf16[1,128,3072]{2,1,0:T(8,128)(2,1)} %bitcast.9) | data formatting | bytes 1572864
  142.9 0.0 copy-done.1
  142.9 0.6 copy.20
  143.5 0.0 copy-done
  143.5 0.6 copy.21
Async XLA Ops:
  139.6 3.3 %copy-start.1 = (f32[24,128]{1,0:T(8,128)S(1)}, f32[24,128]{1,0:T(8,128)}, u32[]{:S(2)}) copy-start(f32[24,128]{1,0:T(8,128)} %get-tuple-element.17) | copy-start | bytes 36868
  139.6 3.9 %copy-start = (f32[24,128]{1,0:T(8,128)S(1)}, f32[24,128]{1,0:T(8,128)}, u32[]{:S(2)}) copy-start(f32[24,128]{1,0:T(8,128)} %get-tuple-element.18) | copy-start | bytes 36868

commit v3 on v2

--- a/solution.py
+++ b/solution.py
@@ -16,7 +16,11 @@
 ROWS_PER_BLOCK = 8
 SAMPLE_STEPS = 16
 RANK = 128
-SPLIT = 1792
+QUARTER = 128
+QUARTER_AT = 0
+CHIPS = ((2, 0), (1, 0), (3, 0), (2, 1), (1, 1), (3, 1), (0, 1))
+COLUMNS = ((1, 0), (3, 0), (2, 1), (0, 1), (1, 1), (3, 1), (2, 0))
+SPLIT = 1536
 
 adapter_scale = 2.0
 adv_floor = 0.5
@@ -64,12 +68,12 @@
 
 def step_kernel(
     n_seq, n_fsdp,
-    hidden_in, q, k, v, noise_in, counts, steps, owners, frozen, down, up, head,
-    final, down_out, up_out, loss_out,
-    hidden, noise, wb, qa, ka, va, oa, ar, noisy, acc, nt, st, na, sa, la, ma, left, sh,
+    hidden_in, q, k, v, noise_in, counts_in, steps_in, owners_in, frozen, down, up, head_in,
+    final_out, down_out, up_out, loss_out,
+    counts, steps, owners, head, final, hidden, noise, wb, qa, ka, va, oa, ar, noisy, acc, nt, st, na, sa, la, ma, left, sh,
     mine, meta, lows, rslots, rewards, slots1, slots2, gt, gslots,
     ksend, krecv, klocal, wsend, wrecv, bsend, brecv, r1s, r1r, r2s, r2r,
-    send, recv, s1, r1, s2, r2, s3, r3,
+    send, recv, lsend, lrecv, s1, r1, s2, r2, s3, r3,
 ):
     t = lax.axis_index("fsdp")
     s = lax.axis_index("seq")
@@ -78,7 +82,8 @@
     length = rows * n_seq
     heads = width // HEAD
     nr = frozen.shape[0]
-    nc = wb.shape[1]
+    nc = wb.shape[3]
+    base = 4 * QUARTER
     own = nr // n_seq
     x, zh, core = t // 4, lax.rem(t // 2, 2), lax.rem(t, 2)
     xp, xm, xo, zz = lax.rem(x + 1, 4), lax.rem(x + 3, 4), lax.rem(x + 2, 4), 1 - zh
@@ -89,6 +94,9 @@
     dev_xp, dev_xm = (place(xp, zh), s), (place(xm, zh), s)
     dev_z = (place(x, zz), lax.rem(s + n_seq // 2, n_seq))
     dev_core = (x * 4 + zh * 2 + 1 - core, s)
+    y, zl = lax.rem(s, 4), s // 4
+    yp, ym, yo = lax.rem(y + 1, 4), lax.rem(y + 3, 4), lax.rem(y + 2, 4)
+    dev_yp, dev_ym = (t, zl * 4 + yp), (t, zl * 4 + ym)
 
     barrier = pltpu.get_barrier_semaphore()
     for axis, count, me in (("seq", n_seq, s), ("fsdp", n_fsdp, t)):
@@ -106,13 +114,17 @@
     wlocal = []
     for j, (part, at, size) in enumerate(((frozen, 0, features), (down, features, RANK),
                                           (up, features + RANK, RANK))):
-        wlocal.append(pltpu.make_async_copy(part, wb.at[feat(t), pl.ds(at, size)], klocal.at[j]))
+        wlocal.append(pltpu.make_async_copy(part, wb.at[t // 2, core, :, pl.ds(at, size)], klocal.at[j]))
     klocals = []
     for j, (part, dst) in enumerate(((k, ka), (q, qa), (v, va))):
         klocals.append(pltpu.make_async_copy(part.at[:, span(s, width)], dst.at[span(s, rows), :],
                                              klocal.at[3 + j]))
     hlocal = [pltpu.make_async_copy(hidden_in, hidden, klocal.at[6]),
-              pltpu.make_async_copy(noise_in, noise, klocal.at[7])]
+              pltpu.make_async_copy(noise_in, noise, klocal.at[7]),
+              pltpu.make_async_copy(head_in, head, klocal.at[8]),
+              pltpu.make_async_copy(counts_in, counts, klocal.at[9]),
+              pltpu.make_async_copy(steps_in, steps, klocal.at[10]),
+              pltpu.make_async_copy(owners_in, owners, klocal.at[11])]
     for copy in wlocal + klocals + hlocal:
         copy.start()
     pl.semaphore_wait(barrier, n_seq + n_fsdp - 1)
@@ -120,8 +132,9 @@
     kcopies = []
 
     def scatter(j, part, dst):
-        for offset in range(1, n_seq):
-            peer = lax.rem(s + offset, n_seq)
+        for dy, dz in COLUMNS:
+            peer = lax.rem(zl + dz, 2) * 4 + lax.rem(y + dy, 4)
+            offset = dz * 4 + dy
             copy = remote(part.at[:, span(peer, width)], dst.at[span(s, rows), :],
                           ksend.at[j, offset], krecv.at[j, offset], "seq", peer)
             copy.start()
@@ -129,37 +142,60 @@
 
     half = nr // 2
     whole, first, second = (0, nr), (0, half), (half, half)
-    every, near, far = (0, nc), (0, SPLIT), (SPLIT, nc - SPLIT)
+    every, near, far = (base, nc - base), (base, SPLIT), (base + SPLIT, nc - base - SPLIT)
+    mine_y = (pl.multiple_of(y * QUARTER, 128), QUARTER)
     wcopies = {}
 
-    def pass_on(i, block, part, columns, device):
-        ref = wb.at[pl.ds(pl.multiple_of(block * nr + part[0], 16), part[1]),
-                    pl.ds(columns[0], columns[1])]
+    def start(i, ref, device):
         wcopies[i] = pltpu.make_async_remote_copy(
             src_ref=ref, dst_ref=ref, send_sem=wsend.at[i], recv_sem=wrecv.at[i],
             device_id=device, device_id_type=MESH)
         wcopies[i].start()
 
+    def pass_on(i, block, part, columns, device):
+        start(i, wb.at[block // 2, core, pl.ds(part[0], part[1]), pl.ds(columns[0], columns[1])],
+              device)
+
+    def quarter(i, j, device, chips=(0, 8)):
+        start(i, wb.at[pl.ds(chips[0], chips[1]), core, :,
+                       pl.ds(pl.multiple_of(j * QUARTER, 128), QUARTER)], device)
+
     def arrived(*which):
         for i in which:
             wcopies[i].wait_recv()
 
     scatter(0, k, ka)
     finish(wlocal)
-    pass_on(0, t, whole, every, dev_xp)
-    pass_on(1, t, whole, every, dev_xm)
+    pass_on(22, t, whole, mine_y, dev_z)
+    pass_on(23, t, whole, mine_y, dev_xp)
+    pass_on(24, t, whole, mine_y, dev_xm)
+    pass_on(0, t, first, every, dev_xp)
+    pass_on(1, t, second, every, dev_xm)
     pass_on(2, t, whole, every, dev_z)
     pass_on(3, t, whole, every, dev_core)
     scatter(1, q, qa)
     scatter(2, v, va)
 
-    arrived(0, 1, 2)
+    arrived(22)
+    pass_on(25, place(x, zz), whole, mine_y, dev_xp)
+    pass_on(26, place(x, zz), whole, mine_y, dev_xm)
+    arrived(23, 24)
+    pass_on(27, place(xm, zh), first, mine_y, dev_xp)
+    pass_on(28, place(xp, zh), second, mine_y, dev_xm)
+    pass_on(39, t, second, every, dev_xp)
+    pass_on(40, t, first, every, dev_xm)
+    arrived(25, 26)
+    pass_on(29, place(xm, zz), first, mine_y, dev_xp)
+    pass_on(30, place(xp, zz), second, mine_y, dev_xm)
+    arrived(0, 1)
     pass_on(4, place(xm, zh), first, every, dev_xp)
     pass_on(5, place(xp, zh), second, every, dev_xm)
+    arrived(2)
+    pass_on(6, place(x, zz), whole, near, dev_xp)
+    pass_on(7, place(x, zz), whole, near, dev_xm)
+    arrived(39, 40)
     pass_on(8, place(xm, zh), whole, far, dev_z)
     pass_on(9, place(xp, zh), whole, far, dev_z)
-    pass_on(6, place(x, zz), whole, near, dev_xp)
-    pass_on(7, place(x, zz), whole, near, dev_xm)
     pass_on(10, place(xm, zh), whole, every, dev_core)
     pass_on(11, place(xp, zh), whole, every, dev_core)
     pass_on(12, place(x, zz), whole, every, dev_core)
@@ -188,6 +224,13 @@
         if i < pairs - 1:
             for part in range(2):
                 back_copy(2 * j + part).start()
+        if i == QUARTER_AT:
+            arrived(27, 28, 29, 30)
+            quarter(31, y, dev_yp)
+            quarter(32, y, dev_ym)
+            quarter(33, y, dev_core)
+        if i < pairs - 1:
+            pass
         else:
             back_copy(s + 1 - 2 * lax.rem(s, 2)).start()
     ar[:, span(s, width)] = oa[span(s, rows), :]
@@ -213,13 +256,42 @@
         noised = ((1.0 - level) * value + level * noise[:, here].astype(F32)).astype(BF16)
         noisy[:, here] = noised
         nt[here, :] = noised.T
+    final_copy = pltpu.make_async_copy(final, final_out, klocal.at[12])
+    final_copy.start()
     mine[...] = jnp.broadcast_to(reward / math.sqrt(length), mine.shape)
     rcopies = share("seq", n_seq, mine, rslots, r1s, r1r)
 
-    def slices(j, part, dst, peer):
-        offset = lax.rem(peer - t + n_fsdp, n_fsdp)
-        return remote(part.at[feat(peer), :], dst.at[:, span(t, rows)], send.at[j, offset],
+    chips = n_fsdp // 2
+    seat = span(core * chips + t // 2, rows)
+
+    def chip(dx, dz):
+        return lax.rem(x + dx, 4) * 2 + lax.rem(zh + dz, 2)
+
+    def slices(j, part, dst, dx, dz, dc):
+        peer = chip(dx, dz) * 2 + lax.rem(core + dc, 2)
+        offset = (dx * 2 + dz) * 2 + dc
+        return remote(part.at[feat(peer), :], dst.at[:, seat], send.at[j, offset],
                       recv.at[j, offset], "fsdp", peer)
+
+    others = [(dx, dz, dc) for dx, dz in CHIPS for dc in range(2)] + [(0, 0, 1)]
+
+    def to_chips(j):
+        copies = []
+        for dx, dz in CHIPS:
+            peer = chip(dx, dz) * 2 + core
+            offset = dx * 2 + dz
+            copy = remote(lows.at[j], la.at[j, core, :, span(t // 2, rows)], lsend.at[j, offset],
+                          lrecv.at[j, offset], "fsdp", peer)
+            copy.start()
+            copies.append(copy)
+        la[j, core, :, span(t // 2, rows)] = lows[j]
+        return copies
+
+    def to_core(j):
+        copy = remote(la.at[j, core], la.at[j, core], lsend.at[j, 0], lrecv.at[j, 0], "fsdp",
+                      t + 1 - 2 * core)
+        copy.start()
+        return [copy]
 
     def spread(j, part, dst):
         copies = []
@@ -230,19 +302,27 @@
             copies.append(copy)
         return copies
 
-    for offset in range(1, n_fsdp):
-        slices(0, nt, na, lax.rem(t + offset, n_fsdp)).start()
-    na[:, span(t, rows)] = nt[feat(t), :]
-
-    tile = (features + RANK) // 5
+
+    tiles = [(c, min(512, features + RANK - c)) for c in range(base, features + RANK, 512)]
 
     def multiply(a, b, start=False):
         here = span(a * 2 + b, 2 * nr)
-        for c in range(5):
-            cols = slice(c * tile, (c + 1) * tile)
-            part = jnp.dot(noisy[:, here], wb[here, cols], preferred_element_type=F32)
+        for at, size in tiles:
+            cols = slice(at, at + size)
+            rhs = wb[a * 2 + b, :, :, cols].reshape(2 * nr, size)
+            part = jnp.dot(noisy[:, here], rhs, preferred_element_type=F32)
             acc[:, cols] = part if start else acc[:, cols] + part
 
+    def multiply_quarter(j):
+        cols = pl.ds(pl.multiple_of(j * QUARTER, 128), QUARTER)
+        rhs = wb[:, :, :, cols].reshape(features, QUARTER)
+        acc[:, cols] = jnp.dot(noisy[...], rhs, preferred_element_type=F32)
+
+    arrived(31, 32)
+    quarter(34, ym, dev_yp, (0, 4))
+    quarter(35, yp, dev_ym, (4, 4))
+    quarter(36, ym, dev_core)
+    quarter(37, yp, dev_core)
     arrived(3)
     multiply(x, zh, True)
     arrived(6, 7)
@@ -250,6 +330,9 @@
     pass_on(16, place(xp, zz), second, near, dev_xm)
     pass_on(17, place(xm, zz), whole, near, dev_core)
     pass_on(18, place(xp, zz), whole, near, dev_core)
+    for other in others:
+        slices(0, nt, na, *other).start()
+    na[:, seat] = nt[feat(t), :]
     finish(rcopies)
     total = rslots[0]
     for c in range(1, n_seq):
@@ -267,8 +350,16 @@
     multiply(x, zz)
     arrived(14)
     multiply(xo, zh)
+    arrived(33)
+    multiply_quarter(y)
     arrived(13, 15, 16)
     pass_on(21, place(xo, zz), whole, every, dev_core)
+    arrived(36)
+    multiply_quarter(ym)
+    arrived(37)
+    multiply_quarter(yp)
+    arrived(34, 35)
+    quarter(38, yo, dev_core)
     arrived(17, 19)
     multiply(xm, zz)
     arrived(18, 20)
@@ -282,69 +373,85 @@
     advantage = jnp.sum(jnp.where(lane == t, advantage, 0.0), axis=1, keepdims=True)
     arrived(21)
     multiply(xo, zz)
+    arrived(38)
+    multiply_quarter(yo)
 
     lowrank = acc[:, features:].astype(BF16)
     lows[1] = lowrank.T
-    low_copies = spread(2, lows.at[1], la.at[1, :, span(t, rows)])
-    la[1, :, span(t, rows)] = lows[1]
+    low_copies = to_chips(1)
     loss = jnp.zeros((rows, 1), F32)
     back = jnp.zeros((rows, RANK), F32)
-    chips = n_fsdp // 2
-    for i in range(chips):
-        j = lax.rem(t // 2 + 1 + i, chips)
+    for dx, dz in CHIPS + ((0, 0),):
+        j = chip(dx, dz)
         here = span(j, 2 * nr)
-        up_rows = wb[here, features + RANK:]
+        up_rows = wb[j, :, :, features + RANK:].reshape(2 * nr, RANK)
         target = noise[:, here].astype(F32) - final[:, here].astype(F32)
         error = acc[:, here] + adapter_scale * lax.dot_general(
             lowrank, up_rows, (((1,), (1,)), ((), ())), preferred_element_type=F32) - target
         loss = loss + jnp.sum(error * error, axis=1, keepdims=True)
         slope = (advantage * error / length).astype(BF16)
         st[here, :] = slope.T
-        if i < chips - 1:
-            for part in range(2):
-                slices(1, st, sa, 2 * j + part).start()
-        else:
-            slices(1, st, sa, t + 1 - 2 * core).start()
+        for dc in range(0 if dx or dz else 1, 2):
+            slices(1, st, sa, dx, dz, dc).start()
         back = back + jnp.dot(slope, up_rows, preferred_element_type=F32)
-    sa[:, span(t, rows)] = st[feat(t), :]
+    sa[:, seat] = st[feat(t), :]
     lows[0] = (adapter_scale * back).astype(BF16).T
-    low_copies += spread(3, lows.at[0], la.at[0, :, span(t, rows)])
-    la[0, :, span(t, rows)] = lows[0]
+    back_copies = to_chips(0)
     token_loss = jnp.broadcast_to(advantage * loss / (features * rows), (rows, 128)).T
     sub = lax.broadcasted_iota(jnp.int32, (8, rows), 0)
-    meta[...] = jnp.where(sub == 0, owners[...], token_loss[0:8, :])
-    low_copies += spread(4, meta, ma.at[:, span(t, rows)])
-    ma[:, span(t, rows)] = meta[...]
+    of_token = lax.broadcasted_iota(jnp.int32, (8, rows), 1) // ROWS_PER_BLOCK
+    named = jnp.zeros((8, rows), jnp.int32)
+    for b in range(rows // ROWS_PER_BLOCK):
+        named = jnp.where(of_token == b, owners[b], named)
+    named = named.astype(F32)
+    meta[...] = jnp.where(sub == 0, named, token_loss[0:8, :])
+    meta_copies = spread(2, meta, ma.at[:, seat])
+    ma[:, seat] = meta[...]
 
     lanes = lax.broadcasted_iota(jnp.int32, (8, 128), 1)
     batch = 4
     norms = jnp.zeros((8, 128), F32)
     finish(low_copies)
-    for offset in range(1, n_fsdp):
-        slices(0, nt, na, lax.rem(t + offset, n_fsdp)).wait()
-        slices(1, st, sa, lax.rem(t + offset, n_fsdp)).wait()
+    low_copies = to_core(1)
+    finish(meta_copies)
     owner = ma[0:1, :]
     loss_out[...] = jnp.broadcast_to(
         jnp.sum(jnp.where(owner == t.astype(F32), ma[1:2, :], 0.0), axis=1, keepdims=True),
         loss_out.shape)
-    for j, other in ((1, sa), (0, na)):
-        for g in range(n_fsdp // batch):
-            for e in range(batch):
-                hot = jnp.where(owner == float(g * batch + e), 1.0, 0.0)
-                hot = jnp.broadcast_to(hot, (16, owner.shape[1])).astype(BF16)
+
+    def shards(j, g, other, norms):
+        for e in range(batch):
+            hot = jnp.where(owner == float(g * batch + e), 1.0, 0.0)
+            hot = jnp.broadcast_to(hot, (16, owner.shape[1])).astype(BF16)
+            for c in range(2):
+                cols = slice(c * chips * rows, (c + 1) * chips * rows)
                 for r in range(RANK // 16):
-                    left[j, e * RANK + r * 16:e * RANK + r * 16 + 16, :] = (
-                        la[j, r * 16:r * 16 + 16, :] * hot)
-            prod = lax.dot_general(left[j], other[...], (((1,), (1,)), ((), ())),
-                                   preferred_element_type=F32)
-            if j == 1:
-                prod = adapter_scale * prod
-            for e in range(batch):
-                piece = prod[e * RANK:(e + 1) * RANK]
-                d = g * batch + e
-                sh[d, j * RANK:(j + 1) * RANK, :] = piece
-                square = jnp.sum(jnp.sum(piece * piece, axis=0, keepdims=True), axis=1, keepdims=True)
-                norms = jnp.where(lanes == d, norms + square, norms)
+                    left[j, e * RANK + r * 16:e * RANK + r * 16 + 16, cols] = (
+                        la[j, c, r * 16:r * 16 + 16, :] * hot[:, cols])
+        prod = lax.dot_general(left[j], other[...], (((1,), (1,)), ((), ())),
+                               preferred_element_type=F32)
+        if j == 1:
+            prod = adapter_scale * prod
+        for e in range(batch):
+            piece = prod[e * RANK:(e + 1) * RANK]
+            d = g * batch + e
+            sh[d, j * RANK:(j + 1) * RANK, :] = piece
+            square = jnp.sum(jnp.sum(piece * piece, axis=0, keepdims=True), axis=1, keepdims=True)
+            norms = jnp.where(lanes == d, norms + square, norms)
+        return norms
+
+    for other in others:
+        slices(1, st, sa, *other).wait()
+    finish(back_copies)
+    back_copies = to_core(0)
+    finish(low_copies)
+    for g in range(n_fsdp // batch):
+        norms = shards(1, g, sa, norms)
+    for other in others:
+        slices(0, nt, na, *other).wait()
+    finish(back_copies)
+    for g in range(n_fsdp // batch):
+        norms = shards(0, g, na, norms)
 
     mine[...] = norms
     finish(share("fsdp", n_fsdp, mine, slots1, s1, r1))
@@ -383,6 +490,29 @@
     up_out[...] = total[:, RANK:]
     for i in range(len(wcopies)):
         wcopies[i].wait_send()
+    final_copy.wait()
+
+
+def hand_over_kernel(final_in, down_in, up_in, loss_in, final, down_out, up_out, loss_out):
+    final[...] = final_in[...]
+    down_out[...] = down_in[...]
+    up_out[...] = up_in[...]
+    loss_out[...] = loss_in[0:1, 0:1]
+
+
+def hand_over(final, grad_down, grad_up, loss):
+    vmem = pl.BlockSpec(memory_space=pltpu.VMEM)
+    return pl.pallas_call(
+        hand_over_kernel,
+        out_shape=(
+            jax.ShapeDtypeStruct(final.shape, final.dtype),
+            jax.ShapeDtypeStruct(grad_down.shape, F32),
+            jax.ShapeDtypeStruct(grad_up.shape, F32),
+            jax.ShapeDtypeStruct((1, 1), F32),
+        ),
+        in_specs=[vmem] * 4,
+        out_specs=(vmem,) * 4,
+    )(final, grad_down, grad_up, loss)
 
 
 def per_device(
@@ -398,9 +528,7 @@
     own = part // n_seq
     length = rows * n_seq
     every = rows * n_fsdp
-    owners = jnp.repeat(block_shard_owner[0, :, 0], ROWS_PER_BLOCK).astype(F32)[None, :]
     vmem = pl.BlockSpec(memory_space=pltpu.VMEM)
-    smem = pl.BlockSpec(memory_space=pltpu.SMEM)
     hbm = pl.BlockSpec(memory_space=pl.ANY)
     dma = pltpu.SemaphoreType.DMA
     final, grad_down, grad_up, loss = pl.pallas_call(
@@ -411,12 +539,17 @@
             jax.ShapeDtypeStruct((own, RANK), F32),
             jax.ShapeDtypeStruct((8, 128), F32),
         ),
-        in_specs=[hbm, hbm, hbm, hbm, hbm, smem, smem, vmem, hbm, hbm, hbm, vmem],
-        out_specs=(vmem,) * 4,
+        in_specs=[hbm] * 12,
+        out_specs=(hbm, vmem, vmem, vmem),
         scratch_shapes=[
+            pltpu.SMEM(group_trajectory_counts.shape, jnp.int32),
+            pltpu.SMEM(timestep.shape, jnp.int32),
+            pltpu.SMEM((rows // ROWS_PER_BLOCK,), jnp.int32),
+            pltpu.VMEM((1, features), F32),
             pltpu.VMEM((rows, features), BF16),
             pltpu.VMEM((rows, features), BF16),
-            pltpu.VMEM((features, features + 2 * RANK), BF16),
+            pltpu.VMEM((rows, features), BF16),
+            pltpu.VMEM((n_fsdp // 2, 2, part, features + 2 * RANK), BF16),
             pltpu.VMEM((length, width), BF16),
             pltpu.VMEM((length, width), BF16),
             pltpu.VMEM((length, width), BF16),
@@ -428,7 +561,7 @@
             pltpu.VMEM((features, rows), BF16),
             pltpu.VMEM((part, every), BF16),
             pltpu.VMEM((part, every), BF16),
-            pltpu.VMEM((2, RANK, every), BF16),
+            pltpu.VMEM((2, 2, RANK, every // 2), BF16),
             pltpu.VMEM((8, every), F32),
             pltpu.VMEM((2, 4 * RANK, every), BF16),
             pltpu.VMEM((n_fsdp, 2 * RANK, part), F32),
@@ -441,12 +574,13 @@
             pltpu.VMEM((n_seq, 8, 128), F32),
             pltpu.VMEM((part, 2 * RANK), F32),
             pltpu.VMEM((n_seq, own, 2 * RANK), F32),
-            dma((3, n_seq)), dma((3, n_seq)), dma((8,)),
-            dma((22,)), dma((22,)),
+            dma((3, n_seq)), dma((3, n_seq)), dma((13,)),
+            dma((41,)), dma((41,)),
             dma((n_seq,)), dma((n_seq,)),
             dma((n_seq,)), dma((n_seq,)),
             dma((n_fsdp,)), dma((n_fsdp,)),
-            dma((5, n_fsdp)), dma((5, n_fsdp)),
+            dma((3, n_fsdp)), dma((3, n_fsdp)),
+            dma((2, n_fsdp // 2)), dma((2, n_fsdp // 2)),
             dma((n_fsdp,)), dma((n_fsdp,)),
             dma((n_seq,)), dma((n_seq,)),
             dma((n_seq,)), dma((n_seq,)),
@@ -459,10 +593,11 @@
         ),
     )(
         incoming_hidden_state[0], projected_queries[0], projected_keys[0], projected_values[0],
-        training_noise[0], group_trajectory_counts, timestep, owners, frozen_weight,
+        training_noise[0], group_trajectory_counts, timestep, block_shard_owner[0, :, 0], frozen_weight,
         adapter_down_weight, adapter_up_weight, linear_reward_head[None, :],
     )
-    return final[None], grad_down, grad_up, loss[:1, :1]
+    final, grad_down, grad_up, loss = hand_over(final, grad_down, grad_up, loss)
+    return final[None], grad_down, grad_up, loss
 
 
 def solution(mesh):

time: 144 us -> 126 us (0.88)
  Pallas kernels: 138 us -> 125 us
  local copies, waits for them, and re-layouts: 5.15 us -> 0 us
    pallas_call x1, Pallas kernels: 138 us -> 123 us  [per_device(): pl.pallas_call(functools.partial(step_kernel, n_seq, n_fsdp), out_shape=(...]
    unnamed x7 -> x0, local copies, waits for them, and re-layouts: 3.27 us -> none
    pallas_call x0 -> x1, Pallas kernels: none -> 2.09 us  [hand_over(): pl.pallas_call(hand_over_kernel, out_shape=(jax.ShapeDtypeStruct(final.sh...]
where the time goes in v3:
time: 126 us
  Pallas kernels  125 us (99%)
    pallas_call x1, Pallas kernels, per_device(): pl.pallas_call(functools.partial(step_kernel, n_seq, n_fsdp), out_shape=(...  123 us

profile of v3, /device:TPU:0, one launch (start us, length us, event | category | flops | bytes accessed | tf_op | source)
XLA Modules:
  0.0 125.6 jit_solution(9436219053779477791)
XLA Ops:
  0.6 122.9 %shard_map.147 = (bf16[128,3072]{1,0:T(8,128)(2,1)}, f32[24,128]{1,0:T(8,128)}, f32[24,128]{1,0:T(8,128)}, f32[8,128]{1,0:T(8,128)}) custom-call(bf16[128,3072]{1,0:T(8,128)(2,1)} %bitcast.8, bf16[128,3072]{1,0:T(8,128)(2,1)} %bitcast.9, bf16[128,3072]{1,0:T(8,128)(2,1)} %bitcast.10, bf16[128,3072]{1,0:T(8,128)(2,1)} %bitcast.11, ...), custom_call_target="tpu_custom_call" | custom-call | flops 10000000000 | bytes 8388608 | tf_op jit(solution)/shard_map/pallas_call | solution.py:534
  123.5 2.1 %shard_map.148 = (bf16[128,3072]{1,0:T(8,128)(2,1)}, f32[24,128]{1,0:T(8,128)}, f32[24,128]{1,0:T(8,128)}, f32[1,1]{1,0:T(1,128)}) custom-call(bf16[128,3072]{1,0:T(8,128)(2,1)} %get-tuple-element.12.final_in, f32[24,128]{1,0:T(8,128)} %get-tuple-element.13.down_in, f32[24,128]{1,0:T(8,128)} %get-tuple-element.14.up_in, f32[8,128]{1,0:T(8,128)} %get-tuple-element.15.loss_in), custom_call_target="tpu_custom_call" | custom-call | tf_op jit(solution)/shard_map/pallas_call | solution.py:505

commit v4 on v3

--- a/solution.py
+++ b/solution.py
@@ -352,8 +352,10 @@
     multiply(xo, zh)
     arrived(33)
     multiply_quarter(y)
-    arrived(13, 15, 16)
-    pass_on(21, place(xo, zz), whole, every, dev_core)
+    arrived(13)
+    pass_on(41, place(xo, zz), whole, far, dev_core)
+    arrived(15, 16)
+    pass_on(21, place(xo, zz), whole, near, dev_core)
     arrived(36)
     multiply_quarter(ym)
     arrived(37)
@@ -371,7 +373,7 @@
         reward = jnp.where(lane == c, rewards[c, 0:1, :], reward)
     advantage = advantage_row(counts, reward, lane)
     advantage = jnp.sum(jnp.where(lane == t, advantage, 0.0), axis=1, keepdims=True)
-    arrived(21)
+    arrived(21, 41)
     multiply(xo, zz)
     arrived(38)
     multiply_quarter(yo)
@@ -501,7 +503,13 @@
 
 
 def hand_over(final, grad_down, grad_up, loss):
-    vmem = pl.BlockSpec(memory_space=pltpu.VMEM)
+    rows, features = final.shape
+    part = pl.BlockSpec((rows // 4, features), lambda i: (i, 0))
+
+    def whole(shape):
+        return pl.BlockSpec(shape, lambda i: (0, 0))
+
+    shape = grad_down.shape
     return pl.pallas_call(
         hand_over_kernel,
         out_shape=(
@@ -510,8 +518,9 @@
             jax.ShapeDtypeStruct(grad_up.shape, F32),
             jax.ShapeDtypeStruct((1, 1), F32),
         ),
-        in_specs=[vmem] * 4,
-        out_specs=(vmem,) * 4,
+        grid=(4,),
+        in_specs=[part, whole(shape), whole(shape), whole(loss.shape)],
+        out_specs=(part, whole(shape), whole(shape), whole((1, 1))),
     )(final, grad_down, grad_up, loss)
 
 
@@ -575,7 +584,7 @@
             pltpu.VMEM((part, 2 * RANK), F32),
             pltpu.VMEM((n_seq, own, 2 * RANK), F32),
             dma((3, n_seq)), dma((3, n_seq)), dma((13,)),
-            dma((41,)), dma((41,)),
+            dma((42,)), dma((42,)),
             dma((n_seq,)), dma((n_seq,)),
             dma((n_seq,)), dma((n_seq,)),
             dma((n_fsdp,)), dma((n_fsdp,)),

time: 126 us -> 127 us (level)
  no operation moved by 1% of the time
where the time goes in v4:
time: 127 us
  Pallas kernels  126 us (99%)
    pallas_call x1, Pallas kernels, per_device(): pl.pallas_call(functools.partial(step_kernel, n_seq, n_fsdp), out_shape=(...  123 us
    pallas_call x1, Pallas kernels, hand_over(): pl.pallas_call(hand_over_kernel, out_shape=(jax.ShapeDtypeStruct(final.sh...  3.29 us

profile of v4, /device:TPU:0, one launch (start us, length us, event | category | flops | bytes accessed | tf_op | source)
XLA Modules:
  0.0 126.8 jit_solution(7625176233671283697)
XLA Ops:
  0.6 122.8 %shard_map.147 = (bf16[128,3072]{1,0:T(8,128)(2,1)}, f32[24,128]{1,0:T(8,128)}, f32[24,128]{1,0:T(8,128)}, f32[8,128]{1,0:T(8,128)}) custom-call(bf16[128,3072]{1,0:T(8,128)(2,1)} %bitcast.8, bf16[128,3072]{1,0:T(8,128)(2,1)} %bitcast.9, bf16[128,3072]{1,0:T(8,128)(2,1)} %bitcast.10, bf16[128,3072]{1,0:T(8,128)(2,1)} %bitcast.11, ...), custom_call_target="tpu_custom_call" | custom-call | flops 10000000000 | bytes 8388608 | tf_op jit(solution)/shard_map/pallas_call | solution.py:543
  123.5 3.3 %shard_map.148 = (bf16[128,3072]{1,0:T(8,128)(2,1)}, f32[24,128]{1,0:T(8,128)}, f32[24,128]{1,0:T(8,128)}, f32[1,1]{1,0:T(1,128)}) custom-call(bf16[128,3072]{1,0:T(8,128)(2,1)} %get-tuple-element.12.final_in, f32[24,128]{1,0:T(8,128)} %get-tuple-element.13.down_in, f32[24,128]{1,0:T(8,128)} %get-tuple-element.14.up_in, f32[8,128]{1,0:T(8,128)} %get-tuple-element.15.loss_in), custom_call_target="tpu_custom_call" | custom-call | tf_op jit(solution)/shard_map/pallas_call | solution.py:513
